TPU v7x, 128 devices: a whole 4x4x4 slice. The times are simulated.
128 devices in a mesh: dp: 4 (over x_hi, core), tensor: 32 (over y, z, x_lo).
Axes of the slice: x: 4 (x_hi: 2, x_lo: 2; x = x_hi * 2 + x_lo), y: 4, z: 4, core: 2. Of those that a mesh axis runs over, the one named last changes fastest.
Arguments:
- hidden_in: bfloat16 [4096, 8192], P('dp'), may hold values from -6 to 6
- attn_gain: float32 [8192], replicated, may hold values from 0.1 to 1.9
- seg_ids: int32 [4096], P('dp'), may hold values from 0 to 15, never falling along the last dimension, each value on 1 to 512 neighbouring positions
- w_query: bfloat16 [8192, 8192], P(None, 'tensor'), may hold values from -0.0625 to 0.0625
- w_key: bfloat16 [8192, 1024], P(None, 'tensor'), may hold values from -0.0625 to 0.0625
- w_value: bfloat16 [8192, 1024], P(None, 'tensor'), may hold values from -0.0625 to 0.0625
- w_down: bfloat16 [8192, 1024], P('tensor'), may hold values from -0.1875 to 0.1875
- prev_side: bfloat16 [4096, 1024], P(('dp', 'tensor')), may hold values from -6 to 6
- gate_logit: float32 [1024], replicated, may hold values from -2 to 2
- side_gain: float32 [1024], replicated, may hold values from 0.5 to 1.5
- w_in: bfloat16 [1024, 1792], P('tensor'), may hold values from -0.1875 to 0.1875
- w_out: bfloat16 [1792, 1024], P('tensor'), may hold values from -0.125 to 0.125
- d_out: bfloat16 [4096, 1024], P(('dp', 'tensor')), may hold values from -6 to 6
Outputs:
- side_out: bfloat16 [4096, 1024], P(('dp', 'tensor'))
- d_prev: bfloat16 [4096, 1024], P(('dp', 'tensor'))
- g_down: float32 [8192, 1024], P('tensor')
- g_in: float32 [1024, 1792], P('tensor')
- g_out: float32 [1792, 1024], P('tensor')
- g_gain: float32 [1024], P('tensor')
- g_gate: float32 [1024], P('tensor')
Inputs may be any that keep to these rules, and one draw needn't show every extreme that they name: `seg_ids`: segment numbers never fall along the tokens; each document spans at most 512 tokens and one spans exactly that many.
All inputs are finite; a program needn't handle non-finite values.
Results may differ from a plain program's by a relative error of at most 0.022.
Values may be sent and summed in bfloat16 or wider, within the bound.
A program may use at most 128 MiB of HBM per device.

v0:
```python
import jax
import jax.numpy as jnp
from jax import lax
from jax.sharding import PartitionSpec as P

KV = 8
HD = 128


def from_partner(value, axis, apart):
    mask = 2**apart
    pairs = [(source, source ^ mask) for source in range(lax.axis_size(axis))]
    return lax.ppermute(value, axis, pairs)


def positions(seg):
    count = seg.shape[0]
    idx = jnp.arange(count, dtype=jnp.int32)
    change = jnp.concatenate([jnp.ones((1,), dtype=bool), seg[1:] != seg[:-1]])
    start = lax.cummax(jnp.where(change, idx, jnp.zeros_like(idx)), axis=0)
    return (idx - start).astype(jnp.float32)


def rotate(vals, pos):
    half = vals.shape[-1] // 2
    freqs = 10000.0 ** (-jnp.arange(half, dtype=jnp.float32) * 2.0 / vals.shape[-1])
    angle = pos[:, None] * freqs[None, :]
    cosine = jnp.cos(angle)[:, None, :]
    sine = jnp.sin(angle)[:, None, :]
    first = vals[..., :half]
    second = vals[..., half:]
    return jnp.concatenate(
        [first * cosine - second * sine, second * cosine + first * sine], axis=-1
    )


def body(
    hidden_in,
    attn_gain,
    seg_ids,
    w_query,
    w_key,
    w_value,
    w_down,
    prev_side,
    gate_logit,
    side_gain,
    w_in,
    w_out,
    d_out,
):
    count = hidden_in.shape[0]
    xf = hidden_in.astype(jnp.float32)
    scale_rms = lax.rsqrt(jnp.mean(xf * xf, axis=-1, keepdims=True) + 1e-05)
    normed = (xf * scale_rms * attn_gain).astype(jnp.bfloat16)
    query = jnp.dot(normed, w_query, preferred_element_type=jnp.float32)
    key_part = jnp.dot(normed, w_key, preferred_element_type=jnp.float32).astype(jnp.bfloat16)
    value_part = jnp.dot(normed, w_value, preferred_element_type=jnp.float32).astype(jnp.bfloat16)
    local_heads = query.shape[1] // HD
    stacked = jnp.stack([key_part, value_part], axis=0)
    own_rank = lax.axis_index("tensor")
    span = lax.axis_size("tensor") // KV
    for bit in range(span.bit_length() - 1):
        partner = from_partner(stacked, "tensor", bit)
        is_upper = own_rank // (1 << bit) % 2 == 1
        stacked = jnp.where(
            is_upper,
            jnp.concatenate([partner, stacked], axis=2),
            jnp.concatenate([stacked, partner], axis=2),
        )
    key = stacked[0]
    value = stacked[1]
    pos = positions(seg_ids)
    q_rot = rotate(query.reshape(count, local_heads, HD), pos).astype(jnp.bfloat16)
    k_rot = (
        rotate(key.astype(jnp.float32).reshape(count, 1, HD), pos)
        .reshape(count, HD)
        .astype(jnp.bfloat16)
    )
    idx = jnp.arange(count, dtype=jnp.int32)
    allowed = (idx[None, :] <= idx[:, None]) & (seg_ids[None, :] == seg_ids[:, None])
    scores = jnp.einsum("thd,sd->hts", q_rot, k_rot, preferred_element_type=jnp.float32) / jnp.sqrt(
        jnp.float32(HD)
    )
    expo = jnp.where(allowed[None], jnp.exp(scores), jnp.float32(0.0))
    probs = (expo / jnp.sum(expo, axis=-1, keepdims=True)).astype(jnp.bfloat16)
    ctx = jnp.einsum("hts,sd->thd", probs, value, preferred_element_type=jnp.float32).astype(
        jnp.bfloat16
    )
    ctx = ctx.reshape(count, local_heads * HD)
    block = ctx
    down = lax.psum_scatter(
        jnp.dot(block, w_down, preferred_element_type=jnp.float32).astype(jnp.bfloat16),
        "tensor",
        scatter_dimension=0,
        tiled=True,
    ).astype(jnp.float32)
    gate = jax.nn.sigmoid(gate_logit)
    prev = prev_side.astype(jnp.float32)
    mix = gate * down + (1.0 - gate) * prev
    rnorm = lax.rsqrt(jnp.mean(mix * mix, axis=-1, keepdims=True) + 1e-05)
    snorm = (mix * rnorm * side_gain).astype(jnp.bfloat16)
    w_in_all, w_out_all = (
        lax.all_gather(w_in, "tensor", axis=0, tiled=True),
        lax.all_gather(w_out, "tensor", axis=0, tiled=True),
    )
    pre = jnp.dot(snorm, w_in_all, preferred_element_type=jnp.float32)
    hid = jax.nn.silu(pre).astype(jnp.bfloat16)
    side_out = (mix + jnp.dot(hid, w_out_all, preferred_element_type=jnp.float32)).astype(
        jnp.bfloat16
    )
    grad_outer = lax.dot_general(
        hid, d_out, (((0,), (0,)), ((), ())), preferred_element_type=jnp.float32
    )
    dhid = lax.dot_general(
        d_out, w_out_all, (((1,), (1,)), ((), ())), preferred_element_type=jnp.float32
    )
    sigma = jax.nn.sigmoid(pre)
    dpre = (dhid * sigma * (1.0 + pre * (1.0 - sigma))).astype(jnp.bfloat16)
    grad_inner = lax.dot_general(
        snorm, dpre, (((0,), (0,)), ((), ())), preferred_element_type=jnp.float32
    )
    dnorm = lax.dot_general(
        dpre, w_in_all, (((1,), (1,)), ((), ())), preferred_element_type=jnp.float32
    )
    gain_part = jnp.sum(dnorm * mix * rnorm, axis=0)
    scaled = dnorm * side_gain
    dmix = (
        d_out.astype(jnp.float32)
        + rnorm * scaled
        - mix * rnorm**3 * jnp.mean(scaled * mix, axis=-1, keepdims=True)
    )
    gate_part = gate * (1.0 - gate) * jnp.sum(dmix * (down - prev), axis=0)
    d_prev = (dmix * (1.0 - gate)).astype(jnp.bfloat16)
    d_down = (dmix * gate).astype(jnp.bfloat16)
    block = ctx
    down_local = lax.dot_general(
        block,
        lax.all_gather(d_down, "tensor", axis=0, tiled=True),
        (((0,), (0,)), ((), ())),
        preferred_element_type=jnp.float32,
    )
    inner_sum, outer_sum, gain_sum, gate_sum = lax.psum(
        (grad_inner, grad_outer, gain_part, gate_part), ("dp", "tensor")
    )
    g_down = lax.psum(down_local.astype(jnp.bfloat16), "dp").astype(jnp.float32)
    rank = lax.axis_index("tensor")
    g_in = lax.dynamic_slice_in_dim(inner_sum, rank * w_in.shape[0], w_in.shape[0], 0)
    g_out = lax.dynamic_slice_in_dim(outer_sum, rank * w_out.shape[0], w_out.shape[0], 0)
    share = gain_sum.shape[0] // lax.axis_size("tensor")
    g_gain = lax.dynamic_slice_in_dim(gain_sum, rank * share, share, 0)
    g_gate = lax.dynamic_slice_in_dim(gate_sum, rank * share, share, 0)
    return (side_out, d_prev, g_down, g_in, g_out, g_gain, g_gate)


def solution(mesh):
    return jax.shard_map(
        body,
        mesh=mesh,
        in_specs=(
            P("dp", None),
            P(),
            P("dp"),
            P(None, "tensor"),
            P(None, "tensor"),
            P(None, "tensor"),
            P("tensor", None),
            P(("dp", "tensor"), None),
            P(),
            P(),
            P("tensor", None),
            P("tensor", None),
            P(("dp", "tensor"), None),
        ),
        out_specs=(
            P(("dp", "tensor"), None),
            P(("dp", "tensor"), None),
            P("tensor", None),
            P("tensor", None),
            P("tensor", None),
            P("tensor"),
            P("tensor"),
        ),
        check_vma=False,
    )
```

profile of v0, /device:TPU:1, one launch (start us, length us, event | category | flops | bytes accessed | tf_op | source)
XLA Modules:
  0.0 960.2 jit_solution(12051105197614863045)
XLA Ops:
  7.2 0.0 copy-start
  7.2 0.0 reduce-scatter.2.cloned.1.call-start
  7.2 7.6 fusion
  14.9 3.1 copy-done.2
  18.0 5.6 fusion.2
  23.6 5.1 fusion.11
  28.6 0.7 copy-done.1
  29.3 5.1 fusion.10
  34.4 2.3 collective-permute-start
  36.7 0.1 slice_compare_fusion
  36.8 1.6 fusion.4
  38.3 0.1 add_select_fusion
  38.4 0.3 reduce-window.9
  38.7 0.1 slice.36
  38.8 0.1 slice_reduce_fusion
  38.9 0.1 fusion.30
  39.0 9.4 fusion.38
  48.4 0.1 fusion.37
  48.4 0.3 copy.32
  48.8 0.3 copy.31
  49.1 1.9 multiply_cosine_fusion
  51.0 0.1 maximum_select_fusion.1
  51.1 1.7 collective-permute-start.1
  52.8 0.3 subtract_convert_fusion
  53.1 5.3 collective-permute-done.1
  58.4 0.1 maximum_select_fusion
  58.6 1.2 fusion.21
  59.7 2.6 fusion.3
  62.4 0.0 copy-start.11
  62.4 0.0 copy-start.3
  62.4 2.8 fusion.8
  65.2 2.1 convolution_convert_fusion
  67.3 0.0 reduce-scatter.2.cloned.1.call-update
  67.4 0.0 all-gather.4.cloned.1.call-start
  67.4 0.7 all-gather.4.cloned.1.call-update
  68.1 0.0 all-gather.6.cloned.1.call-start
  68.2 0.7 all-gather.6.cloned.1.call-update
  68.8 0.3 all-gather.8.cloned.1.call-start
  69.1 143.5 %reduce-scatter.2.cloned.1.call-done = bf16[32,1024]{1,0:T(8,128)(2,1)} async-done(((bf16[1024,1024]{1,0:T(8,128)(2,1)}), bf16[32,1024]{1,0:T(8,128)(2,1)}) %reduce-scatter.2.cloned.1.call-update) | async-done | bytes 65552 | tf_op jit(solution)/shard_map/reduce_scatter | solution.py:92
  212.7 1.0 multiply_reduce_fusion.2
  213.7 164.7 %all-gather.4.cloned.1.call-done = bf16[1024,1792]{1,0:T(8,128)(2,1)} async-done(((bf16[32,1792]{1,0:T(8,128)(2,1)}), bf16[1024,1792]{1,0:T(8,128)(2,1)}) %all-gather.4.cloned.1.call-update) | async-done | bytes 3670032 | tf_op jit(solution)/shard_map/all_gather | solution.py:104
  378.4 2.9 fusion.35
  381.3 162.7 %all-gather.6.cloned.1.call-done = bf16[1792,1024]{1,0:T(8,128)(2,1)} async-done(((bf16[56,1024]{1,0:T(8,128)(2,1)}), bf16[1792,1024]{1,0:T(8,128)(2,1)}) %all-gather.6.cloned.1.call-update) | async-done | bytes 3670032 | tf_op jit(solution)/shard_map/all_gather | solution.py:105
  543.9 3.2 fusion.7
  547.2 3.3 multiply_reduce_fusion
  550.5 0.1 fusion.29
  550.7 0.7 multiply_convert_fusion.1
  551.3 0.0 all-gather.8.cloned.1.call-update
  551.4 0.0 all-reduce.5.cloned.1.call-start
  551.4 154.1 %all-gather.8.cloned.1.call-done = bf16[1024,1024]{1,0:T(8,128)(2,1)} async-done(((bf16[32,1024]{1,0:T(8,128)(2,1)}), bf16[1024,1024]{1,0:T(8,128)(2,1)}) %all-gather.8.cloned.1.call-update) | async-done | bytes 2097168 | tf_op jit(solution)/shard_map/all_gather | solution.py:139
  705.5 3.1 convolution_convert_fusion.1
  708.6 0.0 all-reduce.5.cloned.1.call-update
  708.6 0.0 all-reduce.7.cloned.1.call-start
  708.7 4.2 fusion.34
  712.8 4.1 fusion.36
  716.9 0.0 all-reduce.7.cloned.1.call-update
  717.0 85.0 %all-reduce = (f32[1024]{0:T(1024)S(1)}, f32[1024]{0:T(1024)S(1)}) all-reduce(f32[1024]{0:T(1024)S(1)} %get-tuple-element.7, f32[1024]{0:T(1024)S(1)} %multiply_multiply_fusion), channel_id=1, replica_groups=mesh['dp'=4,'tensor'=32] {'dp','tensor'}, use_global_device_ids=true, to_apply=%region_11.12 | all-reduce | flops 2048 | bytes 16384 | tf_op jit(solution)/shard_map/psum | solution.py:143
  802.0 0.6 dynamic_slice.14
  802.5 0.6 dynamic_slice.15
  803.1 3.5 fusion.9
  806.6 2.1 convert_element_type.104
  808.7 141.4 %all-reduce.7.cloned.1.call-done = (f32[1024,1792]{1,0:T(8,128)}, f32[1792,1024]{1,0:T(8,128)}) async-done(((f32[1024,1792]{1,0:T(8,128)}, f32[1792,1024]{1,0:T(8,128)}), (f32[1024,1792]{1,0:T(8,128)}, f32[1792,1024]{1,0:T(8,128)})) %all-reduce.7.cloned.1.call-update) | async-done | bytes 14680080 | tf_op jit(solution)/shard_map/psum | solution.py:143
  950.1 1.6 constant_dynamic-slice_fusion.1
  951.7 1.6 constant_dynamic-slice_fusion
  (30 shorter events, 0.2 us)
Async XLA Ops:
  7.2 58.1 %copy-start = (bf16[256,1024]{1,0:T(8,128)(2,1)S(1)}, bf16[256,1024]{1,0:T(8,128)(2,1)}, u32[]{:S(2)}) copy-start(bf16[256,1024]{1,0:T(8,128)(2,1)} %param.19) | copy-start | bytes 1572868
  7.2 205.5 %reduce-scatter.2.cloned.1.call-start = ((), (), s32[]{:S(2)}) async-start(), calls=%async_computation.1 | async-start | bytes 2162688 | tf_op jit(solution)/shard_map/reduce_scatter | solution.py:92
  7.2 10.7 %copy-start.2 = (bf16[1024,8192]{1,0:T(8,128)(2,1)S(1)}, bf16[1024,8192]{1,0:T(8,128)(2,1)}, u32[]{:S(2)}) copy-start(bf16[1024,8192]{1,0:T(8,128)(2,1)} %param.13) | copy-start | bytes 50331652
  18.0 5.6 copy-start.7
  23.6 5.7 copy-start.1
  23.6 5.7 copy-start.8
  29.3 7.4 copy-start.10
  34.4 16.6 %collective-permute-start = (bf16[2,1024,32]{1,2,0:T(8,128)(2,1)S(1)}, bf16[2,1024,32]{1,2,0:T(8,128)(2,1)S(1)}, u32[]{:S(2)}, u32[]{:S(2)}) collective-permute-start(bf16[2,1024,32]{1,2,0:T(8,128)(2,1)S(1)} %pad_maximum_fusion), channel_id=1, source_target_pairs={{0,1},{1,0},{2,3},{3,2},{4,5},{5,4},{6,7},{7,6},{8,9},{9,8},{10,11... | collective-permute-start | bytes 393224 | tf_op jit(solution)/shard_map/ppermute | solution.py:13
  49.1 10.6 %copy-start.5 = (pred[1024,1024]{0,1:T(8,128)(4,1)S(1)}, pred[1024,1024]{0,1:T(8,128)(4,1)}, u32[]{:S(2)}) copy-start(pred[1024,1024]{0,1:T(8,128)(4,1)} %fusion.4) | copy-start | bytes 3145732
  51.1 7.3 collective-permute-start.1
  62.4 6.7 copy-start.11
  62.4 150.3 %copy-start.3 = (bf16[32,1024]{1,0:T(8,128)(2,1)S(1)}, bf16[32,1024]{1,0:T(8,128)(2,1)}, u32[]{:S(2)}) copy-start(bf16[32,1024]{1,0:T(8,128)(2,1)} %param.20) | copy-start | bytes 196612
  62.4 316.0 %copy-start.9 = (f32[1024]{0:T(1024)S(1)}, f32[1024]{0:T(1024)}, u32[]{:S(2)}) copy-start(f32[1024]{0:T(1024)} %param.22) | copy-start | bytes 12292
  65.2 478.7 %copy-start.6 = (bf16[32,1024]{1,0:T(8,128)(2,1)S(1)}, bf16[32,1024]{1,0:T(8,128)(2,1)}, u32[]{:S(2)}) copy-start(bf16[32,1024]{1,0:T(8,128)(2,1)} %param.25) | copy-start | bytes 196612
  67.4 311.0 %all-gather.4.cloned.1.call-start = ((), (), s32[]{:S(2)}) async-start(), calls=%async_computation.2 | async-start | bytes 3784704 | tf_op jit(solution)/shard_map/all_gather | solution.py:104
  68.1 475.8 %all-gather.6.cloned.1.call-start = ((), (), s32[]{:S(2)}) async-start(), calls=%async_computation.3 | async-start | bytes 3784704 | tf_op jit(solution)/shard_map/all_gather | solution.py:105
  68.8 636.7 %all-gather.8.cloned.1.call-start = ((), (), s32[]{:S(2)}) async-start(), calls=%async_computation.4 | async-start | bytes 2162688 | tf_op jit(solution)/shard_map/all_gather | solution.py:139
  212.7 334.5 %copy-start.4 = (bf16[32,1024]{1,0:T(8,128)(2,1)S(1)}, bf16[32,1024]{1,0:T(8,128)(2,1)}, u32[]{:S(2)}) copy-start(bf16[32,1024]{1,0:T(8,128)(2,1)} %reduce-scatter.2.cloned.1.call-done) | copy-start | bytes 196612
  551.4 255.2 %all-reduce.5.cloned.1.call-start = ((), (), s32[]{:S(2)}) async-start(), calls=%async_computation.5 | async-start | bytes 1048576 | tf_op jit(solution)/shard_map/psum | solution.py:146
  708.6 241.5 %all-reduce.7.cloned.1.call-start = ((), (), s32[]{:S(2)}) async-start(), calls=%async_computation.6 | async-start | bytes 29360128 | tf_op jit(solution)/shard_map/psum | solution.py:143
Sparse Core Ops, SparseCore 0:
  67.5 145.1 reduce-scatter.1
  214.4 163.9 all-gather.3
  380.1 163.7 all-gather.5
  551.5 153.9 all-gather.7
  708.7 62.7 all-reduce.4
  777.5 172.5 all-reduce.6
where the time goes:
time: 961 us; the launch traced here: 960 us
  waiting for transfers between devices  773 us (80%)
  blocking collectives  85 us (9%)
  matrix products  51.2 us (5%)
  other arithmetic  22.9 us (2%)
  between operations  14.4 us (1%)
    all_gather x1, waiting for transfers between devices, body(): lax.all_gather(w_in, 'tensor', axis=0, tiled=True)  165 us
    all_gather x1, waiting for transfers between devices, body(): lax.all_gather(w_out, 'tensor', axis=0, tiled=True)  163 us
    all_gather x1, waiting for transfers between devices, body(): lax.all_gather(d_down, 'tensor', axis=0, tiled=True)  154 us
    reduce_scatter x1, waiting for transfers between devices, body(): lax.psum_scatter(jnp.dot(block, w_down, preferred_element_type=jnp.float3...  144 us
    psum x1, waiting for transfers between devices, body(): lax.psum((grad_inner, grad_outer, gain_part, gate_part), ('dp', 'tensor'))  141 us
    psum x1, blocking collectives, body(): lax.psum((grad_inner, grad_outer, gain_part, gate_part), ('dp', 'tensor'))  85 us
  transfers between devices with their start and end apart: 8, of which 6 were waited for; matrix products, arithmetic and copies ran while one was open for 3% of the time, Pallas kernels for 0%

commit v1 on v0

v1 whole, which is shorter than its diff:
```python
import jax
import jax.numpy as jnp
import numpy as np
from jax import lax
from jax.experimental import pallas as pl
from jax.experimental.pallas import tpu as pltpu
from jax.sharding import PartitionSpec as P

MESH = pl.DeviceIdType.MESH
F32 = jnp.float32
BF16 = jnp.bfloat16
D = 8192
HD = 128
T = 1024
NT = 32
NDP = 4
SIDE = 1024
EPS = 1e-5
QSCALE = 1.4426950408889634 / np.sqrt(128.0)


def dot(a, b, dims=((1,), (0,))):
    return lax.dot_general(a, b, (dims, ((), ())), preferred_element_type=F32)


def mo(x, n):
    return pl.multiple_of(x, n)


def loop(lo, hi, fn):
    def step(i, carry):
        fn(i)
        return carry

    lax.fori_loop(lo, hi, step, 0)


def sincos(a):
    n = jnp.floor(a * np.float32(2 / np.pi) + 0.5)
    r = a - n * np.float32(1.5703125)
    r = r - n * np.float32(4.837512969970703125e-4)
    r = r - n * np.float32(7.54978995489188216e-8)
    r2 = r * r
    s = r + r * r2 * (-1.6666654611e-1 + r2 * (8.3321608736e-3 - r2 * 1.9515295891e-4))
    c = 1.0 - 0.5 * r2 + r2 * r2 * (
        4.166664568298827e-2 + r2 * (-1.388731625493765e-3 + r2 * 2.443315711809948e-5)
    )
    m = n.astype(jnp.int32)
    odd = (m & 1) == 1
    sin = jnp.where(odd, c, s)
    cos = jnp.where(odd, s, c)
    sin = jnp.where((m & 2) == 2, -sin, sin)
    cos = jnp.where(((m + 1) & 2) == 2, -cos, cos)
    return sin, cos


def kernel(
    x_hbm, wq_hbm, wk_hbm, wv_hbm, wd_hbm,
    gain, seg, freq, win4, woutp, prev, glogit, sgain, dout,
    o_side, o_dprev, o_gdown, o_gin, o_gout, o_gg,
    xbuf, wq, wk, wv, wkv, wd, acc, ssq, scl, cosb, sinb, startb,
    kvown, kvrecv, qbuf, kbuf, vbuf, ctx, ctxt, dsend, drecv,
    win, wout, dout4, snorm4, dns, dnr, sos, sor, ddall, gdf, gds, gdr, gda,
    gsi, gso, r1i, r1o, a2i, a2o, r2i, r2o, o3i, o3o, r3i, r3o, r4i, r4o,
    gv0, gv1, gv2, gv3,
    lsem, xsem,
    kv_s, kv_r, wi_s, wi_r, wo_s, wo_r, wf_s, wf_r, do_s, do_r, rs_s, rs_r,
    sn_s, sn_r, dn_s, dn_r, so_s, so_r, ag_s, ag_r, dr_s, dr_r, da_s, da_r,
    g1_s, g1_r, g2i_s, g2i_r, g2o_s, g2o_r, g3i_s, g3i_r, g3o_s, g3o_r,
    g4i_s, g4i_r, g4o_s, g4o_r, v1_s, v1_r, v2_s, v2_r, v3_s, v3_r,
):
    d = lax.axis_index("dp")
    t = lax.axis_index("tensor")
    core = d % 2
    xh = d // 2
    q = t // 4
    b = t % 4
    yb = t // 8
    sib = xh * 2 + 1 - core

    def rc(src, dst, ss, rs, dd, tt):
        return pltpu.make_async_remote_copy(
            src_ref=src, dst_ref=dst, send_sem=ss, recv_sem=rs,
            device_id=(dd, tt), device_id_type=MESH,
        )

    ld_wk = pltpu.make_async_copy(wk_hbm, wk, lsem.at[0])
    ld_wv = pltpu.make_async_copy(wv_hbm, wv, lsem.at[1])
    ld_wq = pltpu.make_async_copy(wq_hbm, wq, lsem.at[2])
    ld_wd = pltpu.make_async_copy(wd_hbm, wd, lsem.at[3])
    ld_wk.start()
    ld_wv.start()

    def ldx(i):
        rows = pl.ds(mo(i * 256, 256), 256)
        return pltpu.make_async_copy(x_hbm.at[rows], xbuf.at[rows], xsem.at[i])

    loop(0, 4, lambda i: ldx(i).start())
    ld_wq.start()
    ld_wd.start()

    bar = pltpu.get_barrier_semaphore()

    def sig(dd, tt):
        pl.semaphore_signal(bar, inc=1, device_id=(dd, tt), device_id_type=MESH)

    loop(1, NT, lambda j: sig(d, (t + j) % NT))
    sig(sib, t)
    sig((1 - xh) * 2 + 1 - core, t)
    loop(0, 8, lambda j: sig((1 - xh) * 2 + core, 4 * j + b))

    lane = lax.broadcasted_iota(jnp.int32, (1, 128), 1)
    segrow = seg[...].astype(F32)
    segcol = jnp.transpose(jnp.broadcast_to(segrow, (128, T)), (1, 0))

    cnt = jnp.zeros((T, 128), F32)
    for k in range(T // 128):
        cnt = cnt + jnp.where(segrow[:, 128 * k:128 * k + 128] < segcol, 1.0, 0.0)
    start = jnp.sum(cnt, axis=1, keepdims=True)
    tok = lax.broadcasted_iota(jnp.int32, (T, 128), 0).astype(F32)
    startb[...] = jnp.broadcast_to(start, (T, 128))
    sn, cs = sincos((tok - start) * freq[...])
    cosb[...] = cs
    sinb[...] = jnp.where(lane < 64, -sn, sn)

    ri = lax.broadcasted_iota(jnp.int32, (32, 128), 0)
    ci = lax.broadcasted_iota(jnp.int32, (32, 128), 1)
    ek = jnp.where((ci & 63) == ri, 1.0, 0.0).astype(BF16)
    ev = jnp.where((ci & 63) == ri + 32, 1.0, 0.0).astype(BF16)
    ld_wk.wait()
    ld_wv.wait()

    def mkkv(i):
        rows = pl.ds(mo(i * 1024, 1024), 1024)
        wkv[rows, :] = (dot(wk[rows, :], ek) + dot(wv[rows, :], ev)).astype(BF16)

    loop(0, 8, mkkv)

    pl.semaphore_wait(bar, 41)

    hw = pl.ds(mo(core * 256, 256), 256)
    ho = pl.ds(mo(core * 512, 512), 512)

    def c_win(tt):
        return rc(win4.at[tt % 4, :, hw], win.at[pl.ds(mo(32 * t, 32), 32), hw], wi_s.at[tt], wi_r.at[t], d, tt)

    def c_win_in(ss):
        return rc(win4.at[0, :, hw], win.at[pl.ds(mo(32 * ss, 32), 32), hw], wi_s.at[ss], wi_r.at[ss], d, ss)

    loop(1, NT, lambda j: c_win((t + j) % NT).start())
    win[pl.ds(mo(32 * t, 32), 32), hw] = win4[b, :, hw]
    wb = t // 8
    wj = t % 8

    def c_wout(qq):
        return rc(woutp.at[:, ho], wout.at[pl.ds(mo(64 * wj, 64), 64), ho], wo_s.at[qq], wo_r.at[wj], d, 4 * qq + wb)

    def c_wout_in(jj):
        return rc(woutp.at[:, ho], wout.at[pl.ds(mo(64 * jj, 64), 64), ho], wo_s.at[jj], wo_r.at[jj], d, 8 * b + jj)

    def start_wout(qq):
        @pl.when(4 * qq + wb != t)
        def _():
            c_wout(qq).start()

    loop(0, 8, start_wout)

    @pl.when(wb == b)
    def _():
        @pl.when(q * 4 + wb == t)
        def _():
            wout[pl.ds(mo(64 * wj, 64), 64), ho] = woutp[:, ho]

    def qd(src, dst, ss, rs, j):
        bb = (b + j) % 4
        return rc(src, dst, ss.at[bb], rs.at[b], d, 4 * q + bb)

    def qd_in(src, dst, ss, rs, j):
        bb = (b + j) % 4
        return rc(src, dst, ss.at[bb], rs.at[bb], d, 4 * q + bb)

    own32 = pl.ds(mo(32 * b, 32), 32)
    loop(1, 4, lambda j: qd(dout, dout4.at[own32], do_s, do_r, j).start())
    dout4[own32, :] = dout[...]

    def kv_chunk(i):
        rows = pl.ds(mo(i * 256, 256), 256)
        ldx(i).wait()
        acc[...] = jnp.zeros((256, 128), F32)
        ssq[...] = jnp.zeros((256, 128), F32)

        def kk(k):
            cols = pl.ds(mo(k * 1024, 1024), 1024)
            xb = xbuf[rows, cols].astype(F32)
            sq = xb * xb
            part = sq[:, 0:128]
            for m in range(1, 8):
                part = part + sq[:, 128 * m:128 * m + 128]
            ssq[...] = ssq[...] + part
            xg = (xb * gain[:, cols]).astype(BF16)
            xbuf[rows, cols] = xg
            acc[...] = acc[...] + dot(xg, wkv[cols, :])

        loop(0, 8, kk)
        s = lax.rsqrt(jnp.sum(ssq[...], axis=1, keepdims=True) * (1.0 / D) + EPS)
        sb = jnp.broadcast_to(s, (256, 128))
        scl[rows, :] = sb
        kv = acc[...] * sb
        piece = jnp.where(lane < 64, kv[0:128], kv[128:256]).astype(BF16)
        prow = pl.ds(mo(i * 128, 128), 128)
        kvown[prow, :] = piece
        kvrecv[b, prow, :] = piece
        loop(1, 4, lambda j: rc(
            kvown.at[prow], kvrecv.at[b, prow], kv_s.at[i, (b + j) % 4], kv_r.at[i, b], d, 4 * q + (b + j) % 4
        ).start())

    loop(0, 4, kv_chunk)

    ld_wq.wait()

    def q_chunk(i):
        rows = pl.ds(mo(i * 256, 256), 256)
        qv = dot(xbuf[rows, :], wq[...])
        sb = scl[rows, :] * np.float32(QSCALE)
        co = cosb[rows, :] * sb
        si = sinb[rows, :] * sb
        for h in range(2):
            v = qv[:, 128 * h:128 * h + 128]
            qbuf[h, rows, :] = (v * co + pltpu.roll(v, 64, 1) * si).astype(BF16)

    loop(0, 4, q_chunk)

    def kv_in(i, j):
        bb = (b + j) % 4
        prow = pl.ds(mo(i * 128, 128), 128)
        rc(kvown.at[prow], kvrecv.at[bb, prow], kv_s.at[i, bb], kv_r.at[i, bb], d, 4 * q + bb).wait_recv()

    loop(0, 4, lambda i: loop(1, 4, lambda j: kv_in(i, j)))
    er = lax.broadcasted_iota(jnp.int32, (128, 512), 0)
    ec = lax.broadcasted_iota(jnp.int32, (128, 512), 1)
    base = ((er >> 6) << 8) + (((er >> 5) & 1) << 7) + (er & 31)

    def kv_build(i):
        prow = pl.ds(mo(i * 128, 128), 128)
        m = jnp.zeros((128, 512), F32)
        for bb in range(4):
            sel = jnp.where(ec == base + 32 * bb, 1.0, 0.0).astype(BF16)
            m = m + dot(kvrecv[bb, prow, :], sel)
        for h in range(2):
            rows = pl.ds(mo(i * 256 + h * 128, 128), 128)
            kf = m[:, 256 * h:256 * h + 128]
            kbuf[rows, :] = (kf * cosb[rows, :] + pltpu.roll(kf, 64, 1) * sinb[rows, :]).astype(BF16)
            vbuf[rows, 0:128] = m[:, 256 * h + 128:256 * h + 256].astype(BF16)
            vbuf[rows, 128:256] = jnp.ones((128, 128), BF16)

    loop(0, 4, kv_build)
    ld_wd.wait()

    def rs_dst(i, m):
        return i * 8 + (m + wj) % 8

    def rs_copy(tt):
        return rc(dsend.at[tt], drecv.at[t], rs_s.at[tt], rs_r.at[t], d, tt)

    def attn(j):
        i = (yb + 1 + j) % 4
        rows = pl.ds(mo(i * 256, 256), 256)
        k0 = mo(jnp.maximum(i - 2, 0) * 256, 256)
        keys = pl.ds(k0, 768)
        kw = kbuf[keys, :]
        vw = vbuf[keys, :]
        kidx = lax.broadcasted_iota(jnp.int32, (256, 768), 1) + k0
        qidx = lax.broadcasted_iota(jnp.int32, (256, 768), 0) + i * 256
        lo = startb[rows, 0:1].astype(jnp.int32)
        ok = (kidx <= qidx) & (kidx >= lo)
        for h in range(2):
            sc = dot(qbuf[h, rows, :], kw, ((1,), (1,)))
            p = jnp.where(ok, jnp.exp2(sc), 0.0).astype(BF16)
            o = dot(p, vw)
            ctx[rows, 128 * h:128 * h + 128] = (o[:, 0:128] / o[:, 128:256]).astype(BF16)
        down = dot(ctx[rows, :], wd[...]).astype(BF16)
        for m in range(8):
            dsend[i * 8 + m] = down[32 * m:32 * m + 32, :]

        def go(m):
            tt = rs_dst(i, m)

            @pl.when(tt != t)
            def _():
                rs_copy(tt).start()

        loop(0, 8, go)

    loop(0, 4, attn)
    drecv[t] = dsend[t]

    loop(1, NT, lambda j: c_win_in((t + j) % NT).wait_recv())

    def wait_wout(jj):
        @pl.when(8 * b + jj != t)
        def _():
            c_wout_in(jj).wait_recv()

    loop(0, 8, wait_wout)
    fw1 = rc(win.at[:, hw], win.at[:, hw], wf_s.at[0], wf_r.at[0], sib, t)
    fw2 = rc(wout.at[:, ho], wout.at[:, ho], wf_s.at[1], wf_r.at[1], sib, t)
    fw1.start()
    fw2.start()

    def ctx_t(i):
        rows = pl.ds(mo(i * 256, 256), 256)
        ctxt[:, rows] = jnp.transpose(ctx[rows, :].astype(F32), (1, 0)).astype(BF16)

    loop(0, 4, ctx_t)
    loop(1, 4, lambda j: qd_in(dout, dout4.at[pl.ds(mo(32 * ((b + j) % 4), 32), 32)], do_s, do_r, j).wait_recv())
    fw1.wait_recv()
    fw2.wait_recv()
    dhid = dot(dout4[...], wout[...], ((1,), (1,)))

    loop(1, NT, lambda j: rc(
        dsend.at[(t + j) % NT], drecv.at[(t + j) % NT], rs_s.at[(t + j) % NT], rs_r.at[(t + j) % NT], d, (t + j) % NT
    ).wait_recv())
    down = lax.fori_loop(0, NT, lambda s, a: a + drecv[s].astype(F32), jnp.zeros((32, SIDE), F32))
    gate = jax.nn.sigmoid(glogit[...])
    prv = prev[...].astype(F32)
    mix = gate * down + (1.0 - gate) * prv
    r = lax.rsqrt(jnp.mean(mix * mix, axis=1, keepdims=True) + EPS)
    snorm4[own32, :] = (mix * r * sgain[...]).astype(BF16)
    loop(1, 4, lambda j: qd(snorm4.at[own32], snorm4.at[own32], sn_s, sn_r, j).start())

    def in32(j):
        return pl.ds(mo(32 * ((b + j) % 4), 32), 32)

    loop(1, 4, lambda j: qd_in(snorm4.at[in32(j)], snorm4.at[in32(j)], sn_s, sn_r, j).wait_recv())

    sn4 = snorm4[...]
    pre = dot(sn4, win[...])
    sig_pre = jax.nn.sigmoid(pre)
    hid = (pre * sig_pre).astype(BF16)
    dpre = (dhid * sig_pre * (1.0 + pre * (1.0 - sig_pre))).astype(BF16)
    dnp = dot(dpre, win[...], ((1,), (1,))).astype(BF16)
    for bb in range(4):
        dns[bb] = dnp[32 * bb:32 * bb + 32, :]
    loop(1, 4, lambda j: qd(dns.at[(b + j) % 4], dnr.at[b], dn_s, dn_r, j).start())
    dnr[b] = dns[b]
    sop = dot(hid, wout[...]).astype(BF16)
    for bb in range(4):
        sos[bb] = sop[32 * bb:32 * bb + 32, :]
    loop(1, 4, lambda j: qd(sos.at[(b + j) % 4], sor.at[b], so_s, so_r, j).start())
    sor[b] = sos[b]
    gin_l = dot(sn4, dpre, ((0,), (0,))).astype(BF16)
    for dd in range(4):
        gsi[dd] = gin_l[:, 128 * dd:128 * dd + 128]
    gout_l = dot(hid, dout4[...], ((0,), (0,))).astype(BF16)
    for dd in range(4):
        gso[dd] = gout_l[:, 256 * dd:256 * dd + 256]

    loop(1, 4, lambda j: qd_in(dns.at[0], dnr.at[(b + j) % 4], dn_s, dn_r, j).wait_recv())
    dn = (dnr[0].astype(F32) + dnr[1].astype(F32)) + (dnr[2].astype(F32) + dnr[3].astype(F32))
    scaled = dn * sgain[...]
    dmix = (
        dout[...].astype(F32)
        + r * scaled
        - mix * (r * r * r) * jnp.mean(scaled * mix, axis=1, keepdims=True)
    )
    dd_rows = pl.ds(mo(32 * t, 32), 32)
    ddall[dd_rows, :] = (dmix * gate).astype(BF16)
    loop(1, NT, lambda j: rc(
        ddall.at[dd_rows], ddall.at[dd_rows], ag_s.at[(t + j) % NT], ag_r.at[t], d, (t + j) % NT
    ).start())
    o_dprev[...] = (dmix * (1.0 - gate)).astype(BF16)
    gv0[b, :, 0:SIDE] = jnp.sum(dn * mix * r, axis=0, keepdims=True)
    gv0[b, :, SIDE:] = gate * (1.0 - gate) * jnp.sum(dmix * (down - prv), axis=0, keepdims=True)
    loop(1, 4, lambda j: qd(gv0.at[b], gv0.at[b], v1_s, v1_r, j).start())

    def g1(xx, k):
        if k == 0:
            return rc(gsi.at[2 * xx + 1 - core], r1i.at[xx], g1_s.at[0, xx], g1_r.at[0, xx], sib, t)
        return rc(gso.at[2 * xx + 1 - core], r1o.at[xx], g1_s.at[1, xx], g1_r.at[1, xx], sib, t)

    for k in range(2):
        for xx in range(2):
            g1(xx, k).start()

    loop(1, 4, lambda j: qd_in(sos.at[0], sor.at[(b + j) % 4], so_s, so_r, j).wait_recv())
    o_side[...] = (
        mix + ((sor[0].astype(F32) + sor[1].astype(F32)) + (sor[2].astype(F32) + sor[3].astype(F32)))
    ).astype(BF16)

    loop(1, 4, lambda j: qd_in(gv0.at[0], gv0.at[(b + j) % 4], v1_s, v1_r, j).wait_recv())
    gv1[...] = (gv0[0] + gv0[1]) + (gv0[2] + gv0[3])
    cv2 = rc(gv1, gv2, v2_s, v2_r, sib, t)
    cv2.start()

    for xx in range(2):
        g1(xx, 0).wait_recv()
        a2i[xx] = (gsi[2 * xx + core].astype(F32) + r1i[xx].astype(F32)).astype(BF16)
    for xx in range(2):
        g1(xx, 1).wait_recv()
        a2o[xx] = (gso[2 * xx + core].astype(F32) + r1o[xx].astype(F32)).astype(BF16)
    cv2.wait_recv()
    me16 = xh * 8 + q
    gv3[me16] = gv1[...] + gv2[...]

    def peer(j):
        return (me16 + j) % 16

    def g2(p, src, k):
        xx = p // 8
        qq = p % 8
        dev = (2 * xx + core, 4 * qq + b)
        if k == 0:
            return rc(a2i.at[xx, pl.ds(mo(128 * qq, 128), 128)], r2i.at[src], g2i_s.at[p], g2i_r.at[src], *dev)
        if k == 1:
            return rc(a2o.at[xx, pl.ds(mo(64 * qq, 64), 64)], r2o.at[src], g2o_s.at[p], g2o_r.at[src], *dev)
        return rc(gv3.at[me16], gv3.at[src], v3_s.at[p], v3_r.at[src], *dev)

    for k in range(3):
        loop(1, 16, lambda j, k=k: g2(peer(j), me16, k).start())
    r2i[me16] = a2i[xh, pl.ds(mo(128 * q, 128), 128), :]
    r2o[me16] = a2o[xh, pl.ds(mo(64 * q, 64), 64), :]

    loop(1, NT, lambda j: rc(
        ddall.at[dd_rows], ddall.at[pl.ds(mo(32 * ((t + j) % NT), 32), 32)], ag_s.at[(t + j) % NT], ag_r.at[(t + j) % NT], d, (t + j) % NT
    ).wait_recv())
    gdf[...] = dot(ctxt[...], ddall[...]).astype(BF16)

    def dpc(src, dst, ss, rs, slot, j):
        dd = (d + j) % 4
        return rc(src, dst, ss.at[dd], rs.at[slot], dd, t)

    def q64(dd):
        return pl.ds(mo(64 * dd, 64), 64)

    loop(1, 4, lambda j: dpc(gdf.at[q64((d + j) % 4)], gdr.at[d], dr_s, dr_r, d, j).start())
    gdr[d] = gdf[q64(d), :]

    for k in range(3):
        loop(1, 16, lambda j, k=k: g2(peer(j), peer(j), k).wait_recv())
    oi = lax.fori_loop(0, 16, lambda s, a: a + r2i[s].astype(F32), jnp.zeros((128, 128), F32))
    oo = lax.fori_loop(0, 16, lambda s, a: a + r2o[s].astype(F32), jnp.zeros((64, 256), F32))
    o3i[...] = oi.astype(BF16)
    o3o[...] = oo.astype(BF16)
    r3i[b] = o3i[own32, :]
    loop(1, 4, lambda j: qd(o3i.at[in32(j)], r3i.at[b], g3i_s, g3i_r, j).start())
    to_t = 8 * b + q
    from_t = 4 * wj + wb
    co3 = rc(o3o, r3o, g3o_s, g3o_r, d, to_t)

    @pl.when(to_t != t)
    def _():
        co3.start()

    @pl.when(to_t == t)
    def _():
        r3o[...] = o3o[...]

    o_gg[...] = lax.fori_loop(0, 16, lambda s, a: a + gv3[s], jnp.zeros((1, 2 * SIDE), F32))

    loop(1, 4, lambda j: dpc(gdf.at[q64(d)], gdr.at[(d + j) % 4], dr_s, dr_r, (d + j) % 4, j).wait_recv())
    gda[q64(d), :] = (
        (gdr[0].astype(F32) + gdr[1].astype(F32)) + (gdr[2].astype(F32) + gdr[3].astype(F32))
    ).astype(BF16)
    loop(1, 4, lambda j: dpc(gda.at[q64(d)], gda.at[q64(d)], da_s, da_r, d, j).start())

    loop(1, 4, lambda j: qd_in(o3i.at[own32], r3i.at[(b + j) % 4], g3i_s, g3i_r, j).wait_recv())

    @pl.when(from_t != t)
    def _():
        rc(o3o, r3o, g3o_s, g3o_r, d, from_t).wait_recv()

    r4i[d] = r3i[...]
    r4o[d] = r3o[...]
    loop(1, 4, lambda j: dpc(r4i.at[d], r4i.at[d], g4i_s, g4i_r, d, j).start())
    loop(1, 4, lambda j: dpc(r4o.at[d], r4o.at[d], g4o_s, g4o_r, d, j).start())

    loop(1, 4, lambda j: dpc(gda.at[q64(d)], gda.at[q64((d + j) % 4)], da_s, da_r, (d + j) % 4, j).wait_recv())
    o_gdown[...] = gda[...].astype(F32)
    loop(1, 4, lambda j: dpc(r4i.at[d], r4i.at[(d + j) % 4], g4i_s, g4i_r, (d + j) % 4, j).wait_recv())
    loop(1, 4, lambda j: dpc(r4o.at[d], r4o.at[(d + j) % 4], g4o_s, g4o_r, (d + j) % 4, j).wait_recv())
    for dd in range(4):
        for bb in range(4):
            o_gin[:, 512 * bb + 128 * dd:512 * bb + 128 * dd + 128] = r4i[dd, bb].astype(F32)
        o_gout[:, 256 * dd:256 * dd + 256] = r4o[dd].astype(F32)

    loop(1, NT, lambda j: c_win((t + j) % NT).wait_send())

    def wout_sent(qq):
        @pl.when(4 * qq + wb != t)
        def _():
            c_wout(qq).wait_send()

    loop(0, 8, wout_sent)
    fw1.wait_send()
    fw2.wait_send()
    loop(1, 4, lambda j: qd(dout, dout4.at[own32], do_s, do_r, j).wait_send())

    def kv_sent(i):
        prow = pl.ds(mo(i * 128, 128), 128)
        loop(1, 4, lambda j: rc(
            kvown.at[prow], kvrecv.at[b, prow], kv_s.at[i, (b + j) % 4], kv_r.at[i, b], d, 4 * q + (b + j) % 4
        ).wait_send())

    loop(0, 4, kv_sent)
    loop(1, NT, lambda j: rs_copy((t + j) % NT).wait_send())
    loop(1, 4, lambda j: qd(snorm4.at[own32], snorm4.at[own32], sn_s, sn_r, j).wait_send())
    loop(1, 4, lambda j: qd(dns.at[(b + j) % 4], dnr.at[b], dn_s, dn_r, j).wait_send())
    loop(1, 4, lambda j: qd(sos.at[(b + j) % 4], sor.at[b], so_s, so_r, j).wait_send())
    loop(1, NT, lambda j: rc(
        ddall.at[dd_rows], ddall.at[dd_rows], ag_s.at[(t + j) % NT], ag_r.at[t], d, (t + j) % NT
    ).wait_send())
    loop(1, 4, lambda j: qd(gv0.at[b], gv0.at[b], v1_s, v1_r, j).wait_send())
    for k in range(2):
        for xx in range(2):
            g1(xx, k).wait_send()
    cv2.wait_send()
    for k in range(3):
        loop(1, 16, lambda j, k=k: g2(peer(j), me16, k).wait_send())
    loop(1, 4, lambda j: dpc(gdf.at[q64((d + j) % 4)], gdr.at[d], dr_s, dr_r, d, j).wait_send())
    loop(1, 4, lambda j: qd(o3i.at[in32(j)], r3i.at[b], g3i_s, g3i_r, j).wait_send())

    @pl.when(to_t != t)
    def _():
        co3.wait_send()

    loop(1, 4, lambda j: dpc(gda.at[q64(d)], gda.at[q64(d)], da_s, da_r, d, j).wait_send())
    loop(1, 4, lambda j: dpc(r4i.at[d], r4i.at[d], g4i_s, g4i_r, d, j).wait_send())
    loop(1, 4, lambda j: dpc(r4o.at[d], r4o.at[d], g4o_s, g4o_r, d, j).wait_send())


def body(
    hidden_in, attn_gain, seg_ids, w_query, w_key, w_value, w_down,
    prev_side, gate_logit, side_gain, w_in, w_out, d_out,
):
    half = HD // 2
    fr = (10000.0 ** (-np.arange(half) * 2.0 / HD)).astype(np.float32)
    freq = jnp.asarray(np.concatenate([fr, fr])[None])
    win4 = jnp.pad(w_in.reshape(32, 4, 8, 56), ((0, 0), (0, 0), (0, 0), (0, 8)))
    win4 = win4.reshape(32, 4, 512).transpose(1, 0, 2)
    woutp = jnp.pad(w_out, ((0, 8), (0, 0)))
    vm = pl.BlockSpec(memory_space=pltpu.VMEM)
    anym = pl.BlockSpec(memory_space=pl.ANY)
    dma = pltpu.SemaphoreType.DMA

    def V(shape, dt=BF16):
        return pltpu.VMEM(shape, dt)

    scratch = [
        V((T, D)), V((D, 256)), V((D, 32)), V((D, 32)), V((D, 128)), V((256, SIDE)),
        V((256, 128), F32), V((256, 128), F32), V((T, 128), F32), V((T, 128), F32), V((T, 128), F32), V((T, 128), F32),
        V((512, 128)), V((4, 512, 128)), V((2, T, 128)), V((T, 128)), V((T, 256)), V((T, 256)), V((256, T)),
        V((NT, 32, SIDE)), V((NT, 32, SIDE)),
        V((SIDE, 512)), V((512, SIDE)), V((128, SIDE)), V((128, SIDE)),
        V((4, 32, SIDE)), V((4, 32, SIDE)), V((4, 32, SIDE)), V((4, 32, SIDE)),
        V((T, SIDE)), V((256, SIDE)), V((8, 128)), V((4, 64, SIDE)), V((256, SIDE)),
        V((4, SIDE, 128)), V((4, 512, 256)), V((2, SIDE, 128)), V((2, 512, 256)), V((2, SIDE, 128)), V((2, 512, 256)),
        V((16, 128, 128)), V((16, 64, 256)), V((128, 128)), V((64, 256)), V((4, 32, 128)), V((64, 256)),
        V((4, 4, 32, 128)), V((4, 64, 256)),
        V((4, 1, 2 * SIDE), F32), V((1, 2 * SIDE), F32), V((1, 2 * SIDE), F32), V((16, 1, 2 * SIDE), F32),
        dma((4,)), dma((4,)),
        dma((4, 4)), dma((4, 4)), dma((32,)), dma((32,)), dma((8,)), dma((8,)), dma((2,)), dma((2,)),
        dma((4,)), dma((4,)), dma((32,)), dma((32,)),
        dma((4,)), dma((4,)), dma((4,)), dma((4,)), dma((4,)), dma((4,)), dma((32,)), dma((32,)),
        dma((4,)), dma((4,)), dma((4,)), dma((4,)),
        dma((2, 2)), dma((2, 2)), dma((16,)), dma((16,)), dma((16,)), dma((16,)), dma((4,)), dma((4,)), dma, dma,
        dma((4,)), dma((4,)), dma((4,)), dma((4,)), dma((4,)), dma((4,)), dma, dma, dma((16,)), dma((16,)),
    ]
    out = pl.pallas_call(
        kernel,
        out_shape=(
            jax.ShapeDtypeStruct((32, SIDE), BF16),
            jax.ShapeDtypeStruct((32, SIDE), BF16),
            jax.ShapeDtypeStruct((256, SIDE), F32),
            jax.ShapeDtypeStruct((32, 2048), F32),
            jax.ShapeDtypeStruct((64, SIDE), F32),
            jax.ShapeDtypeStruct((1, 2 * SIDE), F32),
        ),
        in_specs=[anym] * 5 + [vm] * 9,
        out_specs=tuple([vm] * 6),
        scratch_shapes=scratch,
        compiler_params=pltpu.CompilerParams(
            collective_id=0, has_side_effects=True, vmem_limit_bytes=60 * 1024 * 1024
        ),
    )(
        hidden_in, w_query, w_key, w_value, w_down,
        attn_gain[None], seg_ids[None], freq, win4, woutp, prev_side, gate_logit[None], side_gain[None], d_out,
    )
    side_out, d_prev, g_down, gin, gout, gg = out
    g_in = gin.reshape(32, 32, 64)[:, :, :56].reshape(32, 1792)
    g_out = gout[:56]
    rank = lax.axis_index("tensor")
    g_gain = lax.dynamic_slice_in_dim(gg[0, :SIDE], rank * 32, 32, 0)
    g_gate = lax.dynamic_slice_in_dim(gg[0, SIDE:], rank * 32, 32, 0)
    return side_out, d_prev, g_down, g_in, g_out, g_gain, g_gate


def solution(mesh):
    return jax.shard_map(
        body,
        mesh=mesh,
        in_specs=(
            P("dp", None), P(), P("dp"), P(None, "tensor"), P(None, "tensor"), P(None, "tensor"),
            P("tensor", None), P(("dp", "tensor"), None), P(), P(), P("tensor", None), P("tensor", None),
            P(("dp", "tensor"), None),
        ),
        out_specs=(
            P(("dp", "tensor"), None), P(("dp", "tensor"), None), P("tensor", None), P("tensor", None),
            P("tensor", None), P("tensor"), P("tensor"),
        ),
        check_vma=False,
    )
```

time: 961 us -> 171 us (0.18)
  the two profiles are of different devices: /device:TPU:1 before, /device:TPU:73 now
where the time goes in v1:
time: 171 us
  Pallas kernels  153 us (89%)
  local copies, waits for them, and re-layouts  17.7 us (10%)
    pallas_call x1, Pallas kernels, body(): pl.pallas_call(kernel, out_shape=(jax.ShapeDtypeStruct((32, SIDE), BF16),...  153 us
    unnamed x9, local copies, waits for them, and re-layouts  10.6 us

profile of v1, /device:TPU:73, one launch (start us, length us, event | category | flops | bytes accessed | tf_op | source)
XLA Modules:
  0.0 171.0 jit_solution(1473655639355419071)
XLA Ops:
  0.6 0.0 copy-start
  0.6 0.0 copy-start.1
  0.7 2.7 %copy.22.wk_hbm = bf16[8192,32]{1,0:T(8,128)(2,1)} copy(bf16[8192,32]{0,1:T(8,128)(2,1)} %param.18) | data formatting | bytes 1048576 | tf_op args[4]
  3.4 2.6 %copy.23.wv_hbm = bf16[8192,32]{1,0:T(8,128)(2,1)} copy(bf16[8192,32]{0,1:T(8,128)(2,1)} %param.19) | data formatting | bytes 1048576 | tf_op args[5]
  6.0 0.0 copy-done
  6.0 0.5 reshape.28
  6.5 0.1 pad.8
  6.6 0.9 reshape.29
  7.5 0.0 copy-done.1
  7.5 0.7 pad.9.woutp
  8.1 152.5 %shard_map.189 = (bf16[32,1024]{1,0:T(8,128)(2,1)}, bf16[32,1024]{1,0:T(8,128)(2,1)}, f32[256,1024]{1,0:T(8,128)}, f32[32,2048]{1,0:T(8,128)}, f32[64,1024]{1,0:T(8,128)}, /*index=5*/f32[1,2048]{1,0:T(1,128)}) custom-call(bf16[1024,8192]{1,0:T(8,128)(2,1)} %x_hbm.1, bf16[8192,256]{1,0:T(8,128)(2,1)} %wq_hbm.1, bf16[8192,32]{1,0:T(8,128)(2,1)} %copy.22.wk_hbm, ...), custom_call_target="tpu_custom_call" | custom-call | tf_op jit(solution)/shard_map/pallas_call | solution.py:568
  160.7 0.7 fusion
  161.4 0.6 dynamic-slice_bitcast_fusion
  161.9 1.1 reshape.30
  163.1 1.0 reshape.31
  164.1 1.6 slice.13
  165.7 1.5 copy.27
  167.2 1.5 copy.28
  168.7 2.3 %copy.29 = f32[256,1024]{1,0:T(8,128)} copy(f32[256,1024]{1,0:T(8,128)} %get-tuple-element.32) | data formatting | bytes 2097152
  (1 shorter events, 0.0 us)
Async XLA Ops:
  0.6 5.4 %copy-start = (bf16[32,1792]{1,0:T(8,128)(2,1)S(1)}, bf16[32,1792]{1,0:T(8,128)(2,1)}, u32[]{:S(2)}) copy-start(bf16[32,1792]{1,0:T(8,128)(2,1)} %param.24) | copy-start | bytes 344068
  0.6 6.8 %copy-start.1 = (bf16[56,1024]{1,0:T(8,128)(2,1)S(1)}, bf16[56,1024]{1,0:T(8,128)(2,1)}, u32[]{:S(2)}) copy-start(bf16[56,1024]{1,0:T(8,128)(2,1)} %param.25) | copy-start | bytes 344068

commit v2 on v1

--- a/solution.py
+++ b/solution.py
@@ -58,14 +58,14 @@
     x_hbm, wq_hbm, wk_hbm, wv_hbm, wd_hbm,
     gain, seg, freq, win4, woutp, prev, glogit, sgain, dout,
     o_side, o_dprev, o_gdown, o_gin, o_gout, o_gg,
-    xbuf, wq, wk, wv, wkv, wd, acc, ssq, scl, cosb, sinb, startb,
-    kvown, kvrecv, qbuf, kbuf, vbuf, ctx, ctxt, dsend, drecv,
-    win, wout, dout4, snorm4, dns, dnr, sos, sor, ddall, gdf, gds, gdr, gda,
+    xbuf, wq, wk, wv, wkv, wd4, acc, accq, ssq, cosb, sinb, startb,
+    kvown, kvrecv, qbuf, kbuf, vbuf, csend, ctx4, ctxt, dsend, drecv,
+    win, wout, dout4, snorm4, dns, dnr, sos, sor, ddall, gds, h1r, h2s, h2r, gda,
     gsi, gso, r1i, r1o, a2i, a2o, r2i, r2o, o3i, o3o, r3i, r3o, r4i, r4o,
     gv0, gv1, gv2, gv3,
     lsem, xsem,
-    kv_s, kv_r, wi_s, wi_r, wo_s, wo_r, wf_s, wf_r, do_s, do_r, rs_s, rs_r,
-    sn_s, sn_r, dn_s, dn_r, so_s, so_r, ag_s, ag_r, dr_s, dr_r, da_s, da_r,
+    kv_s, kv_r, wi_s, wi_r, wo_s, wo_r, wf_s, wf_r, do_s, do_r, rs_s, rs_r, wd_s, wd_r, wg_s, wg_r, ca_s, ca_r,
+    sn_s, sn_r, dn_s, dn_r, so_s, so_r, ag_s, ag_r, h1_s, h1_r, h2_s, h2_r, da_s, da_r,
     g1_s, g1_r, g2i_s, g2i_r, g2o_s, g2o_r, g3i_s, g3i_r, g3o_s, g3o_r,
     g4i_s, g4i_r, g4o_s, g4o_r, v1_s, v1_r, v2_s, v2_r, v3_s, v3_r,
 ):
@@ -87,7 +87,8 @@
     ld_wk = pltpu.make_async_copy(wk_hbm, wk, lsem.at[0])
     ld_wv = pltpu.make_async_copy(wv_hbm, wv, lsem.at[1])
     ld_wq = pltpu.make_async_copy(wq_hbm, wq, lsem.at[2])
-    ld_wd = pltpu.make_async_copy(wd_hbm, wd, lsem.at[3])
+    ld_wd = pltpu.make_async_copy(wd_hbm, wd4.at[yb], lsem.at[3])
+    ld_wd.start()
     ld_wk.start()
     ld_wv.start()
 
@@ -95,9 +96,8 @@
         rows = pl.ds(mo(i * 256, 256), 256)
         return pltpu.make_async_copy(x_hbm.at[rows], xbuf.at[rows], xsem.at[i])
 
-    loop(0, 4, lambda i: ldx(i).start())
     ld_wq.start()
-    ld_wd.start()
+    ldx(0).start()
 
     bar = pltpu.get_barrier_semaphore()
 
@@ -109,10 +109,68 @@
     sig((1 - xh) * 2 + 1 - core, t)
     loop(0, 8, lambda j: sig((1 - xh) * 2 + core, 4 * j + b))
 
+    ld_wd.wait()
+    pl.semaphore_wait(bar, 41)
+
+    t8 = t % 8
+    hr = pl.ds(mo(128 * core, 128), 128)
+
+    def yr(src, dst, ss, rs, j):
+        yy = (yb + j) % 4
+        return rc(src, dst, ss.at[yy], rs.at[yb], d, 8 * yy + t8)
+
+    def yr_in(src, dst, ss, rs, j):
+        yy = (yb + j) % 4
+        return rc(src, dst, ss.at[yy], rs.at[yy], d, 8 * yy + t8)
+
+    def c_wd(j):
+        return yr(wd4.at[yb, hr], wd4.at[yb, hr], wd_s, wd_r, j)
+
+    loop(1, 4, lambda j: c_wd(j).start())
+
+    def c_win(tt):
+        return rc(win4.at[tt % 4, core], win.at[core, pl.ds(mo(32 * t, 32), 32)], wi_s.at[tt], wi_r.at[t], d, tt)
+
+    def c_win_in(ss):
+        return rc(win4.at[0, core], win.at[core, pl.ds(mo(32 * ss, 32), 32)], wi_s.at[ss], wi_r.at[ss], d, ss)
+
+    wb = t // 8
+    wj = t % 8
+
+    def c_wout(qq):
+        return rc(woutp.at[core], wout.at[core, pl.ds(mo(64 * wj, 64), 64)], wo_s.at[qq], wo_r.at[wj], d, 4 * qq + wb)
+
+    def c_wout_in(jj):
+        return rc(woutp.at[core], wout.at[core, pl.ds(mo(64 * jj, 64), 64)], wo_s.at[jj], wo_r.at[jj], d, 8 * b + jj)
+
+    def start_wout(j):
+        qq = (q + j) % 8
+
+        @pl.when(4 * qq + wb != t)
+        def _():
+            c_wout(qq).start()
+
+    loop(0, 8, start_wout)
+
+    @pl.when(wb == b)
+    def _():
+        wout[core, pl.ds(mo(64 * wj, 64), 64), :] = woutp[core]
+
+    def qd(src, dst, ss, rs, j):
+        bb = (b + j) % 4
+        return rc(src, dst, ss.at[bb], rs.at[b], d, 4 * q + bb)
+
+    def qd_in(src, dst, ss, rs, j):
+        bb = (b + j) % 4
+        return rc(src, dst, ss.at[bb], rs.at[bb], d, 4 * q + bb)
+
+    own32 = pl.ds(mo(32 * b, 32), 32)
+    loop(1, 4, lambda j: qd(dout, dout4.at[own32], do_s, do_r, j).start())
+    dout4[own32, :] = dout[...]
+
     lane = lax.broadcasted_iota(jnp.int32, (1, 128), 1)
     segrow = seg[...].astype(F32)
     segcol = jnp.transpose(jnp.broadcast_to(segrow, (128, T)), (1, 0))
-
     cnt = jnp.zeros((T, 128), F32)
     for k in range(T // 128):
         cnt = cnt + jnp.where(segrow[:, 128 * k:128 * k + 128] < segcol, 1.0, 0.0)
@@ -123,88 +181,53 @@
     cosb[...] = cs
     sinb[...] = jnp.where(lane < 64, -sn, sn)
 
-    ri = lax.broadcasted_iota(jnp.int32, (32, 128), 0)
-    ci = lax.broadcasted_iota(jnp.int32, (32, 128), 1)
-    ek = jnp.where((ci & 63) == ri, 1.0, 0.0).astype(BF16)
-    ev = jnp.where((ci & 63) == ri + 32, 1.0, 0.0).astype(BF16)
     ld_wk.wait()
     ld_wv.wait()
-
-    def mkkv(i):
+    gk = (wk[...].astype(F32) * gain[...]).astype(BF16)
+    gvw = (wv[...].astype(F32) * gain[...]).astype(BF16)
+    wkv[0:32, :] = gk
+    wkv[32:64, :] = gvw
+    wkv[64:96, :] = gk
+    wkv[96:128, :] = gvw
+    ld_wq.wait()
+
+    def gain_q(i):
         rows = pl.ds(mo(i * 1024, 1024), 1024)
-        wkv[rows, :] = (dot(wk[rows, :], ek) + dot(wv[rows, :], ev)).astype(BF16)
-
-    loop(0, 8, mkkv)
-
-    pl.semaphore_wait(bar, 41)
-
-    hw = pl.ds(mo(core * 256, 256), 256)
-    ho = pl.ds(mo(core * 512, 512), 512)
-
-    def c_win(tt):
-        return rc(win4.at[tt % 4, :, hw], win.at[pl.ds(mo(32 * t, 32), 32), hw], wi_s.at[tt], wi_r.at[t], d, tt)
-
-    def c_win_in(ss):
-        return rc(win4.at[0, :, hw], win.at[pl.ds(mo(32 * ss, 32), 32), hw], wi_s.at[ss], wi_r.at[ss], d, ss)
-
-    loop(1, NT, lambda j: c_win((t + j) % NT).start())
-    win[pl.ds(mo(32 * t, 32), 32), hw] = win4[b, :, hw]
-    wb = t // 8
-    wj = t % 8
-
-    def c_wout(qq):
-        return rc(woutp.at[:, ho], wout.at[pl.ds(mo(64 * wj, 64), 64), ho], wo_s.at[qq], wo_r.at[wj], d, 4 * qq + wb)
-
-    def c_wout_in(jj):
-        return rc(woutp.at[:, ho], wout.at[pl.ds(mo(64 * jj, 64), 64), ho], wo_s.at[jj], wo_r.at[jj], d, 8 * b + jj)
-
-    def start_wout(qq):
-        @pl.when(4 * qq + wb != t)
-        def _():
-            c_wout(qq).start()
-
-    loop(0, 8, start_wout)
-
-    @pl.when(wb == b)
-    def _():
-        @pl.when(q * 4 + wb == t)
-        def _():
-            wout[pl.ds(mo(64 * wj, 64), 64), ho] = woutp[:, ho]
-
-    def qd(src, dst, ss, rs, j):
-        bb = (b + j) % 4
-        return rc(src, dst, ss.at[bb], rs.at[b], d, 4 * q + bb)
-
-    def qd_in(src, dst, ss, rs, j):
-        bb = (b + j) % 4
-        return rc(src, dst, ss.at[bb], rs.at[bb], d, 4 * q + bb)
-
-    own32 = pl.ds(mo(32 * b, 32), 32)
-    loop(1, 4, lambda j: qd(dout, dout4.at[own32], do_s, do_r, j).start())
-    dout4[own32, :] = dout[...]
+        gcol = jnp.transpose(jnp.broadcast_to(gain[:, rows], (128, 1024)), (1, 0))
+        for h in range(2):
+            hh = slice(128 * h, 128 * h + 128)
+            wq[rows, hh] = (wq[rows, hh].astype(F32) * gcol).astype(BF16)
+
+    ldx(1).start()
+    loop(0, 8, gain_q)
 
     def kv_chunk(i):
         rows = pl.ds(mo(i * 256, 256), 256)
         ldx(i).wait()
+
+        @pl.when(i < 2)
+        def _():
+            ldx(i + 2).start()
+
         acc[...] = jnp.zeros((256, 128), F32)
+        accq[...] = jnp.zeros((256, 256), F32)
         ssq[...] = jnp.zeros((256, 128), F32)
 
         def kk(k):
-            cols = pl.ds(mo(k * 1024, 1024), 1024)
-            xb = xbuf[rows, cols].astype(F32)
-            sq = xb * xb
+            cols = pl.ds(mo(k * 2048, 2048), 2048)
+            xb = xbuf[rows, cols]
+            xf = xb.astype(F32)
+            sq = xf * xf
             part = sq[:, 0:128]
-            for m in range(1, 8):
+            for m in range(1, 16):
                 part = part + sq[:, 128 * m:128 * m + 128]
             ssq[...] = ssq[...] + part
-            xg = (xb * gain[:, cols]).astype(BF16)
-            xbuf[rows, cols] = xg
-            acc[...] = acc[...] + dot(xg, wkv[cols, :])
-
-        loop(0, 8, kk)
+            acc[...] = acc[...] + dot(xb, wkv[:, cols], ((1,), (1,)))
+            accq[...] = accq[...] + dot(xb, wq[cols, :])
+
+        loop(0, 4, kk)
         s = lax.rsqrt(jnp.sum(ssq[...], axis=1, keepdims=True) * (1.0 / D) + EPS)
         sb = jnp.broadcast_to(s, (256, 128))
-        scl[rows, :] = sb
         kv = acc[...] * sb
         piece = jnp.where(lane < 64, kv[0:128], kv[128:256]).astype(BF16)
         prow = pl.ds(mo(i * 128, 128), 128)
@@ -213,22 +236,16 @@
         loop(1, 4, lambda j: rc(
             kvown.at[prow], kvrecv.at[b, prow], kv_s.at[i, (b + j) % 4], kv_r.at[i, b], d, 4 * q + (b + j) % 4
         ).start())
-
-    loop(0, 4, kv_chunk)
-
-    ld_wq.wait()
-
-    def q_chunk(i):
-        rows = pl.ds(mo(i * 256, 256), 256)
-        qv = dot(xbuf[rows, :], wq[...])
-        sb = scl[rows, :] * np.float32(QSCALE)
+        sb = sb * np.float32(QSCALE)
         co = cosb[rows, :] * sb
         si = sinb[rows, :] * sb
         for h in range(2):
-            v = qv[:, 128 * h:128 * h + 128]
+            v = accq[:, 128 * h:128 * h + 128]
             qbuf[h, rows, :] = (v * co + pltpu.roll(v, 64, 1) * si).astype(BF16)
 
-    loop(0, 4, q_chunk)
+    loop(0, 4, kv_chunk)
+    loop(1, NT, lambda j: c_win((t + j) % NT).start())
+    win[core, pl.ds(mo(32 * t, 32), 32), :] = win4[b, core]
 
     def kv_in(i, j):
         bb = (b + j) % 4
@@ -254,13 +271,25 @@
             vbuf[rows, 128:256] = jnp.ones((128, 128), BF16)
 
     loop(0, 4, kv_build)
-    ld_wd.wait()
-
-    def rs_dst(i, m):
-        return i * 8 + (m + wj) % 8
-
-    def rs_copy(tt):
-        return rc(dsend.at[tt], drecv.at[t], rs_s.at[tt], rs_r.at[t], d, tt)
+
+    def c_wg(j):
+        yy = (yb + j) % 4
+        return rc(wd4.at[yy, hr], wd4.at[yy, hr], wg_s.at[yy], wg_r.at[yy], sib, t)
+
+    def c_wg_in(j):
+        yy = (yb + j) % 4
+        hs = pl.ds(mo(128 * (1 - core), 128), 128)
+        return rc(wd4.at[yy, hs], wd4.at[yy, hs], wg_s.at[yy], wg_r.at[yy], sib, t)
+
+    def wd_fwd(j):
+        yy = (yb + j) % 4
+        yr_in(wd4.at[yy, hr], wd4.at[yy, hr], wd_s, wd_r, j).wait_recv()
+        c_wg(j).start()
+
+    loop(1, 4, wd_fwd)
+
+    def c_ctx(j):
+        return yr(csend.at[(yb + j) % 4], ctx4.at[yb], ca_s, ca_r, j)
 
     def attn(j):
         i = (yb + 1 + j) % 4
@@ -277,22 +306,33 @@
             sc = dot(qbuf[h, rows, :], kw, ((1,), (1,)))
             p = jnp.where(ok, jnp.exp2(sc), 0.0).astype(BF16)
             o = dot(p, vw)
-            ctx[rows, 128 * h:128 * h + 128] = (o[:, 0:128] / o[:, 128:256]).astype(BF16)
-        down = dot(ctx[rows, :], wd[...]).astype(BF16)
-        for m in range(8):
-            dsend[i * 8 + m] = down[32 * m:32 * m + 32, :]
-
-        def go(m):
-            tt = rs_dst(i, m)
-
-            @pl.when(tt != t)
-            def _():
-                rs_copy(tt).start()
-
-        loop(0, 8, go)
+            csend[i, :, 128 * h:128 * h + 128] = (o[:, 0:128] / o[:, 128:256]).astype(BF16)
+
+        @pl.when(j < 3)
+        def _():
+            c_ctx(j + 1).start()
 
     loop(0, 4, attn)
-    drecv[t] = dsend[t]
+    ctx4[yb] = csend[yb]
+
+    loop(1, 4, lambda j: c_wg_in(j).wait_recv())
+    loop(1, 4, lambda j: yr_in(csend.at[(yb + j) % 4], ctx4.at[(yb + j) % 4], ca_s, ca_r, j).wait_recv())
+    dpart = (
+        (dot(ctx4[0], wd4[0]) + dot(ctx4[1], wd4[1])) + (dot(ctx4[2], wd4[2]) + dot(ctx4[3], wd4[3]))
+    ).astype(BF16)
+    for m in range(8):
+        dsend[m] = dpart[32 * m:32 * m + 32, :]
+
+    def rs_copy(j):
+        m = (t8 + j) % 8
+        return rc(dsend.at[m], drecv.at[t8], rs_s.at[m], rs_r.at[t8], d, 8 * yb + m)
+
+    def rs_in(j):
+        m = (t8 + j) % 8
+        return rc(dsend.at[m], drecv.at[m], rs_s.at[m], rs_r.at[m], d, 8 * yb + m)
+
+    loop(1, 8, lambda j: rs_copy(j).start())
+    drecv[t8] = dsend[t8]
 
     loop(1, NT, lambda j: c_win_in((t + j) % NT).wait_recv())
 
@@ -302,25 +342,22 @@
             c_wout_in(jj).wait_recv()
 
     loop(0, 8, wait_wout)
-    fw1 = rc(win.at[:, hw], win.at[:, hw], wf_s.at[0], wf_r.at[0], sib, t)
-    fw2 = rc(wout.at[:, ho], wout.at[:, ho], wf_s.at[1], wf_r.at[1], sib, t)
+    fw1 = rc(win.at[core], win.at[core], wf_s.at[0], wf_r.at[0], sib, t)
+    fw2 = rc(wout.at[core], wout.at[core], wf_s.at[1], wf_r.at[1], sib, t)
     fw1.start()
     fw2.start()
 
     def ctx_t(i):
-        rows = pl.ds(mo(i * 256, 256), 256)
-        ctxt[:, rows] = jnp.transpose(ctx[rows, :].astype(F32), (1, 0)).astype(BF16)
+        ctxt[i] = jnp.transpose(ctx4[i].astype(F32), (1, 0)).astype(BF16)
 
     loop(0, 4, ctx_t)
     loop(1, 4, lambda j: qd_in(dout, dout4.at[pl.ds(mo(32 * ((b + j) % 4), 32), 32)], do_s, do_r, j).wait_recv())
     fw1.wait_recv()
     fw2.wait_recv()
-    dhid = dot(dout4[...], wout[...], ((1,), (1,)))
-
-    loop(1, NT, lambda j: rc(
-        dsend.at[(t + j) % NT], drecv.at[(t + j) % NT], rs_s.at[(t + j) % NT], rs_r.at[(t + j) % NT], d, (t + j) % NT
-    ).wait_recv())
-    down = lax.fori_loop(0, NT, lambda s, a: a + drecv[s].astype(F32), jnp.zeros((32, SIDE), F32))
+    dhid = dot(dout4[:, 0:512], wout[0], ((1,), (1,))) + dot(dout4[:, 512:1024], wout[1], ((1,), (1,)))
+
+    loop(1, 8, lambda j: rs_in(j).wait_recv())
+    down = lax.fori_loop(0, 8, lambda m, a: a + drecv[m].astype(F32), jnp.zeros((32, SIDE), F32))
     gate = jax.nn.sigmoid(glogit[...])
     prv = prev[...].astype(F32)
     mix = gate * down + (1.0 - gate) * prv
@@ -334,16 +371,16 @@
     loop(1, 4, lambda j: qd_in(snorm4.at[in32(j)], snorm4.at[in32(j)], sn_s, sn_r, j).wait_recv())
 
     sn4 = snorm4[...]
-    pre = dot(sn4, win[...])
+    pre = jnp.concatenate([dot(sn4, win[0]), dot(sn4, win[1])], axis=1)
     sig_pre = jax.nn.sigmoid(pre)
     hid = (pre * sig_pre).astype(BF16)
     dpre = (dhid * sig_pre * (1.0 + pre * (1.0 - sig_pre))).astype(BF16)
-    dnp = dot(dpre, win[...], ((1,), (1,))).astype(BF16)
+    dnp = (dot(dpre[:, 0:256], win[0], ((1,), (1,))) + dot(dpre[:, 256:512], win[1], ((1,), (1,)))).astype(BF16)
     for bb in range(4):
         dns[bb] = dnp[32 * bb:32 * bb + 32, :]
     loop(1, 4, lambda j: qd(dns.at[(b + j) % 4], dnr.at[b], dn_s, dn_r, j).start())
     dnr[b] = dns[b]
-    sop = dot(hid, wout[...]).astype(BF16)
+    sop = jnp.concatenate([dot(hid, wout[0]), dot(hid, wout[1])], axis=1).astype(BF16)
     for bb in range(4):
         sos[bb] = sop[32 * bb:32 * bb + 32, :]
     loop(1, 4, lambda j: qd(sos.at[(b + j) % 4], sor.at[b], so_s, so_r, j).start())
@@ -363,11 +400,18 @@
         + r * scaled
         - mix * (r * r * r) * jnp.mean(scaled * mix, axis=1, keepdims=True)
     )
-    dd_rows = pl.ds(mo(32 * t, 32), 32)
+    dd_rows = pl.ds(mo(32 * t8, 32), 32)
     ddall[dd_rows, :] = (dmix * gate).astype(BF16)
-    loop(1, NT, lambda j: rc(
-        ddall.at[dd_rows], ddall.at[dd_rows], ag_s.at[(t + j) % NT], ag_r.at[t], d, (t + j) % NT
-    ).start())
+
+    def c_ag(j):
+        m = (t8 + j) % 8
+        return rc(ddall.at[dd_rows], ddall.at[dd_rows], ag_s.at[m], ag_r.at[t8], d, 8 * yb + m)
+
+    def c_ag_in(j):
+        m = (t8 + j) % 8
+        return rc(ddall.at[dd_rows], ddall.at[pl.ds(mo(32 * m, 32), 32)], ag_s.at[m], ag_r.at[m], d, 8 * yb + m)
+
+    loop(1, 8, lambda j: c_ag(j).start())
     o_dprev[...] = (dmix * (1.0 - gate)).astype(BF16)
     gv0[b, :, 0:SIDE] = jnp.sum(dn * mix * r, axis=0, keepdims=True)
     gv0[b, :, SIDE:] = gate * (1.0 - gate) * jnp.sum(dmix * (down - prv), axis=0, keepdims=True)
@@ -420,10 +464,34 @@
     r2i[me16] = a2i[xh, pl.ds(mo(128 * q, 128), 128), :]
     r2o[me16] = a2o[xh, pl.ds(mo(64 * q, 64), 64), :]
 
-    loop(1, NT, lambda j: rc(
-        ddall.at[dd_rows], ddall.at[pl.ds(mo(32 * ((t + j) % NT), 32), 32)], ag_s.at[(t + j) % NT], ag_r.at[(t + j) % NT], d, (t + j) % NT
-    ).wait_recv())
-    gdf[...] = dot(ctxt[...], ddall[...]).astype(BF16)
+    loop(1, 8, lambda j: c_ag_in(j).wait_recv())
+
+    def gpart(yy):
+        g = dot(ctxt[yy], ddall[...]).astype(BF16)
+        for dd in range(4):
+            gds[dd, yy] = g[64 * dd:64 * dd + 64, :]
+
+    loop(0, 4, gpart)
+
+    def h1(xx):
+        return rc(gds.at[2 * xx + 1 - core], h1r.at[xx], h1_s.at[xx], h1_r.at[xx], sib, t)
+
+    for xx in range(2):
+        h1(xx).start()
+    for xx in range(2):
+        h1(xx).wait_recv()
+
+        def h1_sum(yy, xx=xx):
+            h2s[xx, yy] = (gds[2 * xx + core, yy].astype(F32) + h1r[xx, yy].astype(F32)).astype(BF16)
+
+        loop(0, 4, h1_sum)
+    me8 = xh * 4 + yb
+
+    def h2(p, src):
+        return rc(h2s.at[p // 4, p % 4], h2r.at[src], h2_s.at[p], h2_r.at[src], 2 * (p // 4) + core, 8 * (p % 4) + t8)
+
+    loop(1, 8, lambda j: h2((me8 + j) % 8, me8).start())
+    h2r[me8] = h2s[xh, yb]
 
     def dpc(src, dst, ss, rs, slot, j):
         dd = (d + j) % 4
@@ -431,9 +499,6 @@
 
     def q64(dd):
         return pl.ds(mo(64 * dd, 64), 64)
-
-    loop(1, 4, lambda j: dpc(gdf.at[q64((d + j) % 4)], gdr.at[d], dr_s, dr_r, d, j).start())
-    gdr[d] = gdf[q64(d), :]
 
     for k in range(3):
         loop(1, 16, lambda j, k=k: g2(peer(j), peer(j), k).wait_recv())
@@ -457,9 +522,9 @@
 
     o_gg[...] = lax.fori_loop(0, 16, lambda s, a: a + gv3[s], jnp.zeros((1, 2 * SIDE), F32))
 
-    loop(1, 4, lambda j: dpc(gdf.at[q64(d)], gdr.at[(d + j) % 4], dr_s, dr_r, (d + j) % 4, j).wait_recv())
-    gda[q64(d), :] = (
-        (gdr[0].astype(F32) + gdr[1].astype(F32)) + (gdr[2].astype(F32) + gdr[3].astype(F32))
+    loop(1, 8, lambda j: h2((me8 + j) % 8, (me8 + j) % 8).wait_recv())
+    gda[q64(d), :] = lax.fori_loop(
+        0, 8, lambda m, a: a + h2r[m].astype(F32), jnp.zeros((64, SIDE), F32)
     ).astype(BF16)
     loop(1, 4, lambda j: dpc(gda.at[q64(d)], gda.at[q64(d)], da_s, da_r, d, j).start())
 
@@ -485,7 +550,9 @@
 
     loop(1, NT, lambda j: c_win((t + j) % NT).wait_send())
 
-    def wout_sent(qq):
+    def wout_sent(j):
+        qq = (q + j) % 8
+
         @pl.when(4 * qq + wb != t)
         def _():
             c_wout(qq).wait_send()
@@ -502,13 +569,14 @@
         ).wait_send())
 
     loop(0, 4, kv_sent)
-    loop(1, NT, lambda j: rs_copy((t + j) % NT).wait_send())
+    loop(1, 4, lambda j: c_wd(j).wait_send())
+    loop(1, 4, lambda j: c_wg(j).wait_send())
+    loop(1, 4, lambda j: c_ctx(j).wait_send())
+    loop(1, 8, lambda j: rs_copy(j).wait_send())
     loop(1, 4, lambda j: qd(snorm4.at[own32], snorm4.at[own32], sn_s, sn_r, j).wait_send())
     loop(1, 4, lambda j: qd(dns.at[(b + j) % 4], dnr.at[b], dn_s, dn_r, j).wait_send())
     loop(1, 4, lambda j: qd(sos.at[(b + j) % 4], sor.at[b], so_s, so_r, j).wait_send())
-    loop(1, NT, lambda j: rc(
-        ddall.at[dd_rows], ddall.at[dd_rows], ag_s.at[(t + j) % NT], ag_r.at[t], d, (t + j) % NT
-    ).wait_send())
+    loop(1, 8, lambda j: c_ag(j).wait_send())
     loop(1, 4, lambda j: qd(gv0.at[b], gv0.at[b], v1_s, v1_r, j).wait_send())
     for k in range(2):
         for xx in range(2):
@@ -516,7 +584,9 @@
     cv2.wait_send()
     for k in range(3):
         loop(1, 16, lambda j, k=k: g2(peer(j), me16, k).wait_send())
-    loop(1, 4, lambda j: dpc(gdf.at[q64((d + j) % 4)], gdr.at[d], dr_s, dr_r, d, j).wait_send())
+    for xx in range(2):
+        h1(xx).wait_send()
+    loop(1, 8, lambda j: h2((me8 + j) % 8, me8).wait_send())
     loop(1, 4, lambda j: qd(o3i.at[in32(j)], r3i.at[b], g3i_s, g3i_r, j).wait_send())
 
     @pl.when(to_t != t)
@@ -535,9 +605,9 @@
     half = HD // 2
     fr = (10000.0 ** (-np.arange(half) * 2.0 / HD)).astype(np.float32)
     freq = jnp.asarray(np.concatenate([fr, fr])[None])
-    win4 = jnp.pad(w_in.reshape(32, 4, 8, 56), ((0, 0), (0, 0), (0, 0), (0, 8)))
-    win4 = win4.reshape(32, 4, 512).transpose(1, 0, 2)
-    woutp = jnp.pad(w_out, ((0, 8), (0, 0)))
+    win4 = jnp.pad(w_in.reshape(32, 32, 56), ((0, 0), (0, 0), (0, 8)))
+    win4 = win4.reshape(32, 4, 2, 256).transpose(1, 2, 0, 3)
+    woutp = jnp.pad(w_out, ((0, 8), (0, 0))).reshape(64, 2, 512).transpose(1, 0, 2)
     vm = pl.BlockSpec(memory_space=pltpu.VMEM)
     anym = pl.BlockSpec(memory_space=pl.ANY)
     dma = pltpu.SemaphoreType.DMA
@@ -546,22 +616,22 @@
         return pltpu.VMEM(shape, dt)
 
     scratch = [
-        V((T, D)), V((D, 256)), V((D, 32)), V((D, 32)), V((D, 128)), V((256, SIDE)),
-        V((256, 128), F32), V((256, 128), F32), V((T, 128), F32), V((T, 128), F32), V((T, 128), F32), V((T, 128), F32),
-        V((512, 128)), V((4, 512, 128)), V((2, T, 128)), V((T, 128)), V((T, 256)), V((T, 256)), V((256, T)),
-        V((NT, 32, SIDE)), V((NT, 32, SIDE)),
-        V((SIDE, 512)), V((512, SIDE)), V((128, SIDE)), V((128, SIDE)),
+        V((T, D)), V((D, 256)), V((32, D)), V((32, D)), V((128, D)), V((4, 256, SIDE)),
+        V((256, 128), F32), V((256, 256), F32), V((256, 128), F32), V((T, 128), F32), V((T, 128), F32), V((T, 128), F32),
+        V((512, 128)), V((4, 512, 128)), V((2, T, 128)), V((T, 128)), V((T, 256)), V((4, 256, 256)), V((4, 256, 256)), V((4, 256, 256)),
+        V((8, 32, SIDE)), V((8, 32, SIDE)),
+        V((2, SIDE, 256)), V((2, 512, 512)), V((128, SIDE)), V((128, SIDE)),
         V((4, 32, SIDE)), V((4, 32, SIDE)), V((4, 32, SIDE)), V((4, 32, SIDE)),
-        V((T, SIDE)), V((256, SIDE)), V((8, 128)), V((4, 64, SIDE)), V((256, SIDE)),
+        V((256, SIDE)), V((4, 4, 64, SIDE)), V((2, 4, 64, SIDE)), V((2, 4, 64, SIDE)), V((8, 64, SIDE)), V((256, SIDE)),
         V((4, SIDE, 128)), V((4, 512, 256)), V((2, SIDE, 128)), V((2, 512, 256)), V((2, SIDE, 128)), V((2, 512, 256)),
         V((16, 128, 128)), V((16, 64, 256)), V((128, 128)), V((64, 256)), V((4, 32, 128)), V((64, 256)),
         V((4, 4, 32, 128)), V((4, 64, 256)),
         V((4, 1, 2 * SIDE), F32), V((1, 2 * SIDE), F32), V((1, 2 * SIDE), F32), V((16, 1, 2 * SIDE), F32),
         dma((4,)), dma((4,)),
         dma((4, 4)), dma((4, 4)), dma((32,)), dma((32,)), dma((8,)), dma((8,)), dma((2,)), dma((2,)),
-        dma((4,)), dma((4,)), dma((32,)), dma((32,)),
-        dma((4,)), dma((4,)), dma((4,)), dma((4,)), dma((4,)), dma((4,)), dma((32,)), dma((32,)),
-        dma((4,)), dma((4,)), dma((4,)), dma((4,)),
+        dma((4,)), dma((4,)), dma((8,)), dma((8,)), dma((4,)), dma((4,)), dma((4,)), dma((4,)), dma((4,)), dma((4,)),
+        dma((4,)), dma((4,)), dma((4,)), dma((4,)), dma((4,)), dma((4,)), dma((8,)), dma((8,)),
+        dma((2,)), dma((2,)), dma((8,)), dma((8,)), dma((4,)), dma((4,)),
         dma((2, 2)), dma((2, 2)), dma((16,)), dma((16,)), dma((16,)), dma((16,)), dma((4,)), dma((4,)), dma, dma,
         dma((4,)), dma((4,)), dma((4,)), dma((4,)), dma((4,)), dma((4,)), dma, dma, dma((16,)), dma((16,)),
     ]
@@ -582,7 +652,7 @@
             collective_id=0, has_side_effects=True, vmem_limit_bytes=60 * 1024 * 1024
         ),
     )(
-        hidden_in, w_query, w_key, w_value, w_down,
+        hidden_in, w_query, w_key.T, w_value.T, w_down,
         attn_gain[None], seg_ids[None], freq, win4, woutp, prev_side, gate_logit[None], side_gain[None], d_out,
     )
     side_out, d_prev, g_down, gin, gout, gg = out

time: 171 us -> 133 us (0.78)
  the two profiles are of different devices: /device:TPU:73 before, /device:TPU:1 now
where the time goes in v2:
time: 133 us; the launch traced here: 131 us
  Pallas kernels  116 us (87%)
  local copies, waits for them, and re-layouts  14.2 us (11%)
    pallas_call x1, Pallas kernels, body(): pl.pallas_call(kernel, out_shape=(jax.ShapeDtypeStruct((32, SIDE), BF16),...  116 us
    unnamed x3, local copies, waits for them, and re-layouts  5.25 us

profile of v2, /device:TPU:1, one launch (start us, length us, event | category | flops | bytes accessed | tf_op | source)
XLA Modules:
  0.0 130.8 jit_solution(14738857855781703951)
XLA Ops:
  0.6 0.9 pad.9
  1.5 0.7 copy.26
  2.2 1.4 %reshape.31 = bf16[32,32,56]{2,1,0:T(8,128)(2,1)S(1)} reshape(bf16[32,1792]{1,0:T(8,128)(2,1)} %param.24) | data formatting | bytes 229376 | tf_op jit(solution)/shard_map/reshape | solution.py:608
  3.6 0.1 pad.8
  3.7 0.2 reshape.32
  3.9 0.7 copy.27
  4.6 115.9 %shard_map.189 = (bf16[32,1024]{1,0:T(8,128)(2,1)}, bf16[32,1024]{1,0:T(8,128)(2,1)}, f32[256,1024]{1,0:T(8,128)}, f32[32,2048]{1,0:T(8,128)}, f32[64,1024]{1,0:T(8,128)}, /*index=5*/f32[1,2048]{1,0:T(1,128)}) custom-call(bf16[1024,8192]{1,0:T(8,128)(2,1)} %x_hbm.1, bf16[8192,256]{1,0:T(8,128)(2,1)} %wq_hbm.1, bf16[32,8192]{1,0:T(8,128)(2,1)} %bitcast.24, ...), custom_call_target="tpu_custom_call" | custom-call | tf_op jit(solution)/shard_map/pallas_call | solution.py:638
  120.5 0.7 fusion
  121.2 0.6 dynamic-slice_bitcast_fusion
  121.7 1.6 %slice.13 = f32[56,1024]{1,0:T(8,128)} slice(f32[64,1024]{1,0:T(8,128)} %get-tuple-element.17), slice={[0:56], [0:1024]} | slice | bytes 458752 | tf_op jit(solution)/shard_map/slice | solution.py:660
  123.4 1.1 reshape.34
  124.5 1.0 reshape.35
  125.5 1.5 %copy.31 = bf16[32,1024]{1,0:T(8,128)(2,1)} copy(bf16[32,1024]{1,0:T(8,128)(2,1)} %get-tuple-element.30) | data formatting | bytes 131072
  127.0 1.5 %copy.32 = bf16[32,1024]{1,0:T(8,128)(2,1)} copy(bf16[32,1024]{1,0:T(8,128)(2,1)} %get-tuple-element.31) | data formatting | bytes 131072
  128.5 2.3 %copy.33 = f32[256,1024]{1,0:T(8,128)} copy(f32[256,1024]{1,0:T(8,128)} %get-tuple-element.32) | data formatting | bytes 2097152

commit v3 on v2

--- a/solution.py
+++ b/solution.py
@@ -56,8 +56,9 @@
 
 def kernel(
     x_hbm, wq_hbm, wk_hbm, wv_hbm, wd_hbm,
-    gain, seg, freq, win4, woutp, prev, glogit, sgain, dout,
-    o_side, o_dprev, o_gdown, o_gin, o_gout, o_gg,
+    gain, seg, freq, w_in, w_out, prev, glogit, sgain, dout,
+    o_side, o_dprev, o_gda, o_r4i, o_r4o, o_gg,
+    win4, woutp, wout2,
     xbuf, wq, wk, wv, wkv, wd4, acc, accq, ssq, cosb, sinb, startb,
     kvown, kvrecv, qbuf, kbuf, vbuf, csend, ctx4, ctxt, dsend, drecv,
     win, wout, dout4, snorm4, dns, dnr, sos, sor, ddall, gds, h1r, h2s, h2r, gda,
@@ -109,6 +110,16 @@
     sig((1 - xh) * 2 + 1 - core, t)
     loop(0, 8, lambda j: sig((1 - xh) * 2 + core, 4 * j + b))
 
+    wif = w_in[...].astype(F32)
+    wir = pltpu.roll(wif, 1792 - 64, 1)
+    for bb in range(4):
+        for h in range(2):
+            c0 = 448 * bb + 256 * h
+            win4[bb, h] = (wif[:, c0:c0 + 256] if bb % 2 == 0 else wir[:, c0 - 64:c0 + 192]).astype(BF16)
+    wof = jnp.concatenate([w_out[...].astype(F32), jnp.zeros((8, SIDE), F32)], axis=0)
+    for h in range(2):
+        woutp[h] = wof[:, 512 * h:512 * h + 512].astype(BF16)
+
     ld_wd.wait()
     pl.semaphore_wait(bar, 41)
 
@@ -354,7 +365,12 @@
     loop(1, 4, lambda j: qd_in(dout, dout4.at[pl.ds(mo(32 * ((b + j) % 4), 32), 32)], do_s, do_r, j).wait_recv())
     fw1.wait_recv()
     fw2.wait_recv()
-    dhid = dot(dout4[:, 0:512], wout[0], ((1,), (1,))) + dot(dout4[:, 512:1024], wout[1], ((1,), (1,)))
+    for h in range(2):
+        wf = wout[h].astype(F32)
+        wout2[h] = jnp.concatenate(
+            [wf[64 * j:64 * j + 56] for j in range(8)] + [jnp.zeros((64, 512), F32)], axis=0
+        ).astype(BF16)
+    dhid = dot(dout4[:, 0:512], wout2[0], ((1,), (1,))) + dot(dout4[:, 512:1024], wout2[1], ((1,), (1,)))
 
     loop(1, 8, lambda j: rs_in(j).wait_recv())
     down = lax.fori_loop(0, 8, lambda m, a: a + drecv[m].astype(F32), jnp.zeros((32, SIDE), F32))
@@ -380,17 +396,26 @@
         dns[bb] = dnp[32 * bb:32 * bb + 32, :]
     loop(1, 4, lambda j: qd(dns.at[(b + j) % 4], dnr.at[b], dn_s, dn_r, j).start())
     dnr[b] = dns[b]
-    sop = jnp.concatenate([dot(hid, wout[0]), dot(hid, wout[1])], axis=1).astype(BF16)
+    sop = jnp.concatenate([dot(hid, wout2[0]), dot(hid, wout2[1])], axis=1).astype(BF16)
     for bb in range(4):
         sos[bb] = sop[32 * bb:32 * bb + 32, :]
-    loop(1, 4, lambda j: qd(sos.at[(b + j) % 4], sor.at[b], so_s, so_r, j).start())
     sor[b] = sos[b]
     gin_l = dot(sn4, dpre, ((0,), (0,))).astype(BF16)
     for dd in range(4):
         gsi[dd] = gin_l[:, 128 * dd:128 * dd + 128]
-    gout_l = dot(hid, dout4[...], ((0,), (0,))).astype(BF16)
+    gout_l = dot(hid, dout4[...], ((0,), (0,)))
     for dd in range(4):
-        gso[dd] = gout_l[:, 256 * dd:256 * dd + 256]
+        for j in range(8):
+            gso[dd, 64 * j:64 * j + 64, :] = gout_l[56 * j:56 * j + 64, 256 * dd:256 * dd + 256].astype(BF16)
+
+    def g1(xx, k):
+        if k == 0:
+            return rc(gsi.at[2 * xx + 1 - core], r1i.at[xx], g1_s.at[0, xx], g1_r.at[0, xx], sib, t)
+        return rc(gso.at[2 * xx + 1 - core], r1o.at[xx], g1_s.at[1, xx], g1_r.at[1, xx], sib, t)
+
+    for k in range(2):
+        for xx in range(2):
+            g1(xx, k).start()
 
     loop(1, 4, lambda j: qd_in(dns.at[0], dnr.at[(b + j) % 4], dn_s, dn_r, j).wait_recv())
     dn = (dnr[0].astype(F32) + dnr[1].astype(F32)) + (dnr[2].astype(F32) + dnr[3].astype(F32))
@@ -412,24 +437,11 @@
         return rc(ddall.at[dd_rows], ddall.at[pl.ds(mo(32 * m, 32), 32)], ag_s.at[m], ag_r.at[m], d, 8 * yb + m)
 
     loop(1, 8, lambda j: c_ag(j).start())
+    loop(1, 4, lambda j: qd(sos.at[(b + j) % 4], sor.at[b], so_s, so_r, j).start())
     o_dprev[...] = (dmix * (1.0 - gate)).astype(BF16)
     gv0[b, :, 0:SIDE] = jnp.sum(dn * mix * r, axis=0, keepdims=True)
     gv0[b, :, SIDE:] = gate * (1.0 - gate) * jnp.sum(dmix * (down - prv), axis=0, keepdims=True)
     loop(1, 4, lambda j: qd(gv0.at[b], gv0.at[b], v1_s, v1_r, j).start())
-
-    def g1(xx, k):
-        if k == 0:
-            return rc(gsi.at[2 * xx + 1 - core], r1i.at[xx], g1_s.at[0, xx], g1_r.at[0, xx], sib, t)
-        return rc(gso.at[2 * xx + 1 - core], r1o.at[xx], g1_s.at[1, xx], g1_r.at[1, xx], sib, t)
-
-    for k in range(2):
-        for xx in range(2):
-            g1(xx, k).start()
-
-    loop(1, 4, lambda j: qd_in(sos.at[0], sor.at[(b + j) % 4], so_s, so_r, j).wait_recv())
-    o_side[...] = (
-        mix + ((sor[0].astype(F32) + sor[1].astype(F32)) + (sor[2].astype(F32) + sor[3].astype(F32)))
-    ).astype(BF16)
 
     loop(1, 4, lambda j: qd_in(gv0.at[0], gv0.at[(b + j) % 4], v1_s, v1_r, j).wait_recv())
     gv1[...] = (gv0[0] + gv0[1]) + (gv0[2] + gv0[3])
@@ -499,6 +511,11 @@
 
     def q64(dd):
         return pl.ds(mo(64 * dd, 64), 64)
+
+    loop(1, 4, lambda j: qd_in(sos.at[0], sor.at[(b + j) % 4], so_s, so_r, j).wait_recv())
+    o_side[...] = (
+        mix + ((sor[0].astype(F32) + sor[1].astype(F32)) + (sor[2].astype(F32) + sor[3].astype(F32)))
+    ).astype(BF16)
 
     for k in range(3):
         loop(1, 16, lambda j, k=k: g2(peer(j), peer(j), k).wait_recv())
@@ -540,13 +557,11 @@
     loop(1, 4, lambda j: dpc(r4o.at[d], r4o.at[d], g4o_s, g4o_r, d, j).start())
 
     loop(1, 4, lambda j: dpc(gda.at[q64(d)], gda.at[q64((d + j) % 4)], da_s, da_r, (d + j) % 4, j).wait_recv())
-    o_gdown[...] = gda[...].astype(F32)
+    o_gda[...] = gda[...]
     loop(1, 4, lambda j: dpc(r4i.at[d], r4i.at[(d + j) % 4], g4i_s, g4i_r, (d + j) % 4, j).wait_recv())
     loop(1, 4, lambda j: dpc(r4o.at[d], r4o.at[(d + j) % 4], g4o_s, g4o_r, (d + j) % 4, j).wait_recv())
-    for dd in range(4):
-        for bb in range(4):
-            o_gin[:, 512 * bb + 128 * dd:512 * bb + 128 * dd + 128] = r4i[dd, bb].astype(F32)
-        o_gout[:, 256 * dd:256 * dd + 256] = r4o[dd].astype(F32)
+    o_r4i[...] = r4i[...]
+    o_r4o[...] = r4o[...]
 
     loop(1, NT, lambda j: c_win((t + j) % NT).wait_send())
 
@@ -598,6 +613,33 @@
     loop(1, 4, lambda j: dpc(r4o.at[d], r4o.at[d], g4o_s, g4o_r, d, j).wait_send())
 
 
+def finish(side, dprev, gda, gi, go, gg, o_side, o_dprev, o_gdown, o_gin, o_gout, o_gain, o_gate):
+    o_side[...] = side[...]
+    o_dprev[...] = dprev[...]
+    o_gdown[...] = gda[...].astype(F32)
+    cols = [None] * 14
+    for bb in range(4):
+        p = jnp.concatenate([gi[dd, bb].astype(F32) for dd in range(4)], axis=1)
+        first = 7 * (bb // 2)
+        if bb % 2 == 1:
+            p = pltpu.roll(p, 64, 1)
+            first += 3
+        for m in range(4):
+            v = p[:, 128 * m:128 * m + 128]
+            cols[first + m] = v if cols[first + m] is None else cols[first + m] + v
+    for m in range(14):
+        o_gin[:, 128 * m:128 * m + 128] = cols[m]
+    for dd in range(4):
+        o_gout[:, 256 * dd:256 * dd + 256] = go[dd].astype(F32)[0:56]
+    t = lax.axis_index("tensor")
+    for k, o in enumerate((o_gain, o_gate)):
+        x = gg[:, pl.ds(mo(k * SIDE + (t // 4) * 128, 128), 128)]
+        v = x[:, 0:32]
+        for m in range(1, 4):
+            v = jnp.where(t % 4 == m, pltpu.roll(x, 128 - 32 * m, 1)[:, 0:32], v)
+        o[...] = v
+
+
 def body(
     hidden_in, attn_gain, seg_ids, w_query, w_key, w_value, w_down,
     prev_side, gate_logit, side_gain, w_in, w_out, d_out,
@@ -605,9 +647,6 @@
     half = HD // 2
     fr = (10000.0 ** (-np.arange(half) * 2.0 / HD)).astype(np.float32)
     freq = jnp.asarray(np.concatenate([fr, fr])[None])
-    win4 = jnp.pad(w_in.reshape(32, 32, 56), ((0, 0), (0, 0), (0, 8)))
-    win4 = win4.reshape(32, 4, 2, 256).transpose(1, 2, 0, 3)
-    woutp = jnp.pad(w_out, ((0, 8), (0, 0))).reshape(64, 2, 512).transpose(1, 0, 2)
     vm = pl.BlockSpec(memory_space=pltpu.VMEM)
     anym = pl.BlockSpec(memory_space=pl.ANY)
     dma = pltpu.SemaphoreType.DMA
@@ -616,6 +655,7 @@
         return pltpu.VMEM(shape, dt)
 
     scratch = [
+        V((4, 2, 32, 256)), V((2, 64, 512)), V((2, 512, 512)),
         V((T, D)), V((D, 256)), V((32, D)), V((32, D)), V((128, D)), V((4, 256, SIDE)),
         V((256, 128), F32), V((256, 256), F32), V((256, 128), F32), V((T, 128), F32), V((T, 128), F32), V((T, 128), F32),
         V((512, 128)), V((4, 512, 128)), V((2, T, 128)), V((T, 128)), V((T, 256)), V((4, 256, 256)), V((4, 256, 256)), V((4, 256, 256)),
@@ -640,9 +680,9 @@
         out_shape=(
             jax.ShapeDtypeStruct((32, SIDE), BF16),
             jax.ShapeDtypeStruct((32, SIDE), BF16),
-            jax.ShapeDtypeStruct((256, SIDE), F32),
-            jax.ShapeDtypeStruct((32, 2048), F32),
-            jax.ShapeDtypeStruct((64, SIDE), F32),
+            jax.ShapeDtypeStruct((256, SIDE), BF16),
+            jax.ShapeDtypeStruct((4, 4, 32, 128), BF16),
+            jax.ShapeDtypeStruct((4, 64, 256), BF16),
             jax.ShapeDtypeStruct((1, 2 * SIDE), F32),
         ),
         in_specs=[anym] * 5 + [vm] * 9,
@@ -653,15 +693,23 @@
         ),
     )(
         hidden_in, w_query, w_key.T, w_value.T, w_down,
-        attn_gain[None], seg_ids[None], freq, win4, woutp, prev_side, gate_logit[None], side_gain[None], d_out,
+        attn_gain[None], seg_ids[None], freq, w_in, w_out, prev_side, gate_logit[None], side_gain[None], d_out,
     )
-    side_out, d_prev, g_down, gin, gout, gg = out
-    g_in = gin.reshape(32, 32, 64)[:, :, :56].reshape(32, 1792)
-    g_out = gout[:56]
-    rank = lax.axis_index("tensor")
-    g_gain = lax.dynamic_slice_in_dim(gg[0, :SIDE], rank * 32, 32, 0)
-    g_gate = lax.dynamic_slice_in_dim(gg[0, SIDE:], rank * 32, 32, 0)
-    return side_out, d_prev, g_down, g_in, g_out, g_gain, g_gate
+    side_out, d_prev, g_down, g_in, g_out, g_gain, g_gate = pl.pallas_call(
+        finish,
+        out_shape=(
+            jax.ShapeDtypeStruct((32, SIDE), BF16),
+            jax.ShapeDtypeStruct((32, SIDE), BF16),
+            jax.ShapeDtypeStruct((256, SIDE), F32),
+            jax.ShapeDtypeStruct((32, 1792), F32),
+            jax.ShapeDtypeStruct((56, SIDE), F32),
+            jax.ShapeDtypeStruct((1, 32), F32),
+            jax.ShapeDtypeStruct((1, 32), F32),
+        ),
+        in_specs=[vm] * 6,
+        out_specs=tuple([vm] * 7),
+    )(*out)
+    return side_out, d_prev, g_down, g_in, g_out, g_gain.reshape(32), g_gate.reshape(32)
 
 
 def solution(mesh):

time: 133 us -> 122 us (0.917)
  local copies, waits for them, and re-layouts: 14.2 us -> 0 us
  Pallas kernels: 116 us -> 119 us
    unnamed x3 -> x0, local copies, waits for them, and re-layouts: 5.25 us -> none
    reshape x6 -> x0, local copies, waits for them, and re-layouts: 5.07 us -> none  [the longest x2 2.12 us: body(): g_in = gin.reshape(32, 32, 64)[:, :, :56].reshape(32, 1792)]
    pallas_call x0 -> x1, Pallas kernels: none -> 2.4 us  [body(): pl.pallas_call(finish, out_shape=(jax.ShapeDtypeStruct((32, SIDE), BF16),...]
    slice x2 -> x0, local copies, waits for them, and re-layouts: 2.32 us -> none  [the longest x1 1.64 us: body(): g_out = gout[:56]]
where the time goes in v3:
time: 122 us; the launch traced here: 120 us
  Pallas kernels  119 us (98%)
    pallas_call x1, Pallas kernels, body(): pl.pallas_call(kernel, out_shape=(jax.ShapeDtypeStruct((32, SIDE), BF16),...  117 us

profile of v3, /device:TPU:1, one launch (start us, length us, event | category | flops | bytes accessed | tf_op | source)
XLA Modules:
  0.0 120.0 jit_solution(8995382042153414145)
XLA Ops:
  0.6 116.9 %shard_map.189 = (bf16[32,1024]{1,0:T(8,128)(2,1)}, bf16[32,1024]{1,0:T(8,128)(2,1)}, bf16[256,1024]{1,0:T(8,128)(2,1)}, bf16[4,4,32,128]{3,2,1,0:T(8,128)(2,1)}...) custom-call(bf16[1024,8192]{1,0:T(8,128)(2,1)} %x_hbm.1, bf16[8192,256]{1,0:T(8,128)(2,1)} %wq_hbm.1, ...), custom_call_target="tpu_custom_call" | custom-call | tf_op jit(solution)/shard_map/pallas_call | solution.py:678
  117.6 2.4 %shard_map.190 = (bf16[32,1024]{1,0:T(8,128)(2,1)}, bf16[32,1024]{1,0:T(8,128)(2,1)}, f32[256,1024]{1,0:T(8,128)}, f32[32,1792]{1,0:T(8,128)}, f32[56,1024]{1,0:...) custom-call(bf16[32,1024]{1,0:T(8,128)(2,1)} %get-tuple-element.20.side, bf16[32,1024]{1,0:T(8,128)(2,1)} %get-tuple-element.21.dprev, ...), custom_call_target="tpu_custom_call" | custom-call | tf_op jit(solution)/shard_map/pallas_call | solution.py:698

commit v4 on v3

--- a/solution.py
+++ b/solution.py
@@ -396,26 +396,16 @@
         dns[bb] = dnp[32 * bb:32 * bb + 32, :]
     loop(1, 4, lambda j: qd(dns.at[(b + j) % 4], dnr.at[b], dn_s, dn_r, j).start())
     dnr[b] = dns[b]
-    sop = jnp.concatenate([dot(hid, wout2[0]), dot(hid, wout2[1])], axis=1).astype(BF16)
-    for bb in range(4):
-        sos[bb] = sop[32 * bb:32 * bb + 32, :]
-    sor[b] = sos[b]
     gin_l = dot(sn4, dpre, ((0,), (0,))).astype(BF16)
     for dd in range(4):
         gsi[dd] = gin_l[:, 128 * dd:128 * dd + 128]
-    gout_l = dot(hid, dout4[...], ((0,), (0,)))
-    for dd in range(4):
-        for j in range(8):
-            gso[dd, 64 * j:64 * j + 64, :] = gout_l[56 * j:56 * j + 64, 256 * dd:256 * dd + 256].astype(BF16)
-
     def g1(xx, k):
         if k == 0:
             return rc(gsi.at[2 * xx + 1 - core], r1i.at[xx], g1_s.at[0, xx], g1_r.at[0, xx], sib, t)
         return rc(gso.at[2 * xx + 1 - core], r1o.at[xx], g1_s.at[1, xx], g1_r.at[1, xx], sib, t)
 
-    for k in range(2):
-        for xx in range(2):
-            g1(xx, k).start()
+    for xx in range(2):
+        g1(xx, 0).start()
 
     loop(1, 4, lambda j: qd_in(dns.at[0], dnr.at[(b + j) % 4], dn_s, dn_r, j).wait_recv())
     dn = (dnr[0].astype(F32) + dnr[1].astype(F32)) + (dnr[2].astype(F32) + dnr[3].astype(F32))
@@ -437,26 +427,21 @@
         return rc(ddall.at[dd_rows], ddall.at[pl.ds(mo(32 * m, 32), 32)], ag_s.at[m], ag_r.at[m], d, 8 * yb + m)
 
     loop(1, 8, lambda j: c_ag(j).start())
-    loop(1, 4, lambda j: qd(sos.at[(b + j) % 4], sor.at[b], so_s, so_r, j).start())
+
+    gout_l = dot(hid, dout4[...], ((0,), (0,)))
+    for dd in range(4):
+        for j in range(8):
+            gso[dd, 64 * j:64 * j + 64, :] = gout_l[56 * j:56 * j + 64, 256 * dd:256 * dd + 256].astype(BF16)
+
+    for xx in range(2):
+        g1(xx, 1).start()
+
     o_dprev[...] = (dmix * (1.0 - gate)).astype(BF16)
     gv0[b, :, 0:SIDE] = jnp.sum(dn * mix * r, axis=0, keepdims=True)
     gv0[b, :, SIDE:] = gate * (1.0 - gate) * jnp.sum(dmix * (down - prv), axis=0, keepdims=True)
     loop(1, 4, lambda j: qd(gv0.at[b], gv0.at[b], v1_s, v1_r, j).start())
 
-    loop(1, 4, lambda j: qd_in(gv0.at[0], gv0.at[(b + j) % 4], v1_s, v1_r, j).wait_recv())
-    gv1[...] = (gv0[0] + gv0[1]) + (gv0[2] + gv0[3])
-    cv2 = rc(gv1, gv2, v2_s, v2_r, sib, t)
-    cv2.start()
-
-    for xx in range(2):
-        g1(xx, 0).wait_recv()
-        a2i[xx] = (gsi[2 * xx + core].astype(F32) + r1i[xx].astype(F32)).astype(BF16)
-    for xx in range(2):
-        g1(xx, 1).wait_recv()
-        a2o[xx] = (gso[2 * xx + core].astype(F32) + r1o[xx].astype(F32)).astype(BF16)
-    cv2.wait_recv()
     me16 = xh * 8 + q
-    gv3[me16] = gv1[...] + gv2[...]
 
     def peer(j):
         return (me16 + j) % 16
@@ -471,53 +456,79 @@
             return rc(a2o.at[xx, pl.ds(mo(64 * qq, 64), 64)], r2o.at[src], g2o_s.at[p], g2o_r.at[src], *dev)
         return rc(gv3.at[me16], gv3.at[src], v3_s.at[p], v3_r.at[src], *dev)
 
-    for k in range(3):
-        loop(1, 16, lambda j, k=k: g2(peer(j), me16, k).start())
+    for xx in range(2):
+        g1(xx, 0).wait_recv()
+        a2i[xx] = (gsi[2 * xx + core].astype(F32) + r1i[xx].astype(F32)).astype(BF16)
+    loop(1, 16, lambda j: g2(peer(j), me16, 0).start())
     r2i[me16] = a2i[xh, pl.ds(mo(128 * q, 128), 128), :]
+    for xx in range(2):
+        g1(xx, 1).wait_recv()
+        a2o[xx] = (gso[2 * xx + core].astype(F32) + r1o[xx].astype(F32)).astype(BF16)
+    loop(1, 16, lambda j: g2(peer(j), me16, 1).start())
     r2o[me16] = a2o[xh, pl.ds(mo(64 * q, 64), 64), :]
 
+    loop(1, 4, lambda j: qd_in(gv0.at[0], gv0.at[(b + j) % 4], v1_s, v1_r, j).wait_recv())
+    gv1[...] = (gv0[0] + gv0[1]) + (gv0[2] + gv0[3])
+    cv2 = rc(gv1, gv2, v2_s, v2_r, sib, t)
+    cv2.start()
+
     loop(1, 8, lambda j: c_ag_in(j).wait_recv())
 
-    def gpart(yy):
+    def h1(xx, yy):
+        return rc(gds.at[2 * xx + 1 - core, yy], h1r.at[xx, yy], h1_s.at[xx, yy], h1_r.at[xx, yy], sib, t)
+
+    def gpart(j):
+        yy = (yb + 1 + j) % 4
         g = dot(ctxt[yy], ddall[...]).astype(BF16)
         for dd in range(4):
             gds[dd, yy] = g[64 * dd:64 * dd + 64, :]
+        for xx in range(2):
+            h1(xx, yy).start()
 
     loop(0, 4, gpart)
-
-    def h1(xx):
-        return rc(gds.at[2 * xx + 1 - core], h1r.at[xx], h1_s.at[xx], h1_r.at[xx], sib, t)
-
-    for xx in range(2):
-        h1(xx).start()
-    for xx in range(2):
-        h1(xx).wait_recv()
-
-        def h1_sum(yy, xx=xx):
-            h2s[xx, yy] = (gds[2 * xx + core, yy].astype(F32) + h1r[xx, yy].astype(F32)).astype(BF16)
-
-        loop(0, 4, h1_sum)
     me8 = xh * 4 + yb
 
     def h2(p, src):
         return rc(h2s.at[p // 4, p % 4], h2r.at[src], h2_s.at[p], h2_r.at[src], 2 * (p // 4) + core, 8 * (p % 4) + t8)
 
-    loop(1, 8, lambda j: h2((me8 + j) % 8, me8).start())
+    def h1_sum(j):
+        yy = (yb + 1 + j) % 4
+        for xx in range(2):
+            h1(xx, yy).wait_recv()
+            h2s[xx, yy] = (gds[2 * xx + core, yy].astype(F32) + h1r[xx, yy].astype(F32)).astype(BF16)
+
+            @pl.when(xx * 4 + yy != me8)
+            def _():
+                h2(xx * 4 + yy, me8).start()
+
+    loop(0, 4, h1_sum)
     h2r[me8] = h2s[xh, yb]
-
-    def dpc(src, dst, ss, rs, slot, j):
-        dd = (d + j) % 4
-        return rc(src, dst, ss.at[dd], rs.at[slot], dd, t)
+    cv2.wait_recv()
+    gv3[me16] = gv1[...] + gv2[...]
+    loop(1, 16, lambda j: g2(peer(j), me16, 2).start())
+    sop = jnp.concatenate([dot(hid, wout2[0]), dot(hid, wout2[1])], axis=1).astype(BF16)
+    for bb in range(4):
+        sos[bb] = sop[32 * bb:32 * bb + 32, :]
+    sor[b] = sos[b]
+    loop(1, 4, lambda j: qd(sos.at[(b + j) % 4], sor.at[b], so_s, so_r, j).start())
+
+    dx = 2 * (1 - xh) + core
+    dy = 2 * (1 - xh) + 1 - core
+
+    def over_dp(at, ss, rs):
+        return dict(
+            sib=rc(at(d), at(d), ss.at[0], rs.at[d], sib, t),
+            x=rc(at(d), at(d), ss.at[1], rs.at[d], dx, t),
+            fwd=rc(at(dx), at(dx), ss.at[2], rs.at[dx], sib, t),
+            in_sib=rc(at(sib), at(sib), ss.at[0], rs.at[sib], sib, t),
+            in_x=rc(at(dx), at(dx), ss.at[1], rs.at[dx], dx, t),
+            in_fwd=rc(at(dy), at(dy), ss.at[2], rs.at[dy], sib, t),
+        )
 
     def q64(dd):
         return pl.ds(mo(64 * dd, 64), 64)
 
-    loop(1, 4, lambda j: qd_in(sos.at[0], sor.at[(b + j) % 4], so_s, so_r, j).wait_recv())
-    o_side[...] = (
-        mix + ((sor[0].astype(F32) + sor[1].astype(F32)) + (sor[2].astype(F32) + sor[3].astype(F32)))
-    ).astype(BF16)
-
-    for k in range(3):
+    for k in range(2):
         loop(1, 16, lambda j, k=k: g2(peer(j), peer(j), k).wait_recv())
     oi = lax.fori_loop(0, 16, lambda s, a: a + r2i[s].astype(F32), jnp.zeros((128, 128), F32))
     oo = lax.fori_loop(0, 16, lambda s, a: a + r2o[s].astype(F32), jnp.zeros((64, 256), F32))
@@ -537,13 +548,14 @@
     def _():
         r3o[...] = o3o[...]
 
-    o_gg[...] = lax.fori_loop(0, 16, lambda s, a: a + gv3[s], jnp.zeros((1, 2 * SIDE), F32))
 
     loop(1, 8, lambda j: h2((me8 + j) % 8, (me8 + j) % 8).wait_recv())
     gda[q64(d), :] = lax.fori_loop(
         0, 8, lambda m, a: a + h2r[m].astype(F32), jnp.zeros((64, SIDE), F32)
     ).astype(BF16)
-    loop(1, 4, lambda j: dpc(gda.at[q64(d)], gda.at[q64(d)], da_s, da_r, d, j).start())
+    tda = over_dp(lambda p: gda.at[q64(p)], da_s, da_r)
+    tda["x"].start()
+    tda["sib"].start()
 
     loop(1, 4, lambda j: qd_in(o3i.at[own32], r3i.at[(b + j) % 4], g3i_s, g3i_r, j).wait_recv())
 
@@ -553,13 +565,24 @@
 
     r4i[d] = r3i[...]
     r4o[d] = r3o[...]
-    loop(1, 4, lambda j: dpc(r4i.at[d], r4i.at[d], g4i_s, g4i_r, d, j).start())
-    loop(1, 4, lambda j: dpc(r4o.at[d], r4o.at[d], g4o_s, g4o_r, d, j).start())
-
-    loop(1, 4, lambda j: dpc(gda.at[q64(d)], gda.at[q64((d + j) % 4)], da_s, da_r, (d + j) % 4, j).wait_recv())
+    t4i = over_dp(lambda p: r4i.at[p], g4i_s, g4i_r)
+    t4o = over_dp(lambda p: r4o.at[p], g4o_s, g4o_r)
+    for c in (t4i, t4o):
+        c["x"].start()
+        c["sib"].start()
+    loop(1, 4, lambda j: qd_in(sos.at[0], sor.at[(b + j) % 4], so_s, so_r, j).wait_recv())
+    o_side[...] = (
+        mix + ((sor[0].astype(F32) + sor[1].astype(F32)) + (sor[2].astype(F32) + sor[3].astype(F32)))
+    ).astype(BF16)
+    loop(1, 16, lambda j: g2(peer(j), peer(j), 2).wait_recv())
+    o_gg[...] = lax.fori_loop(0, 16, lambda s, a: a + gv3[s], jnp.zeros((1, 2 * SIDE), F32))
+    for c in (tda, t4i, t4o):
+        c["in_x"].wait_recv()
+        c["fwd"].start()
+    for c in (tda, t4i, t4o):
+        c["in_sib"].wait_recv()
+        c["in_fwd"].wait_recv()
     o_gda[...] = gda[...]
-    loop(1, 4, lambda j: dpc(r4i.at[d], r4i.at[(d + j) % 4], g4i_s, g4i_r, (d + j) % 4, j).wait_recv())
-    loop(1, 4, lambda j: dpc(r4o.at[d], r4o.at[(d + j) % 4], g4o_s, g4o_r, (d + j) % 4, j).wait_recv())
     o_r4i[...] = r4i[...]
     o_r4o[...] = r4o[...]
 
@@ -600,7 +623,7 @@
     for k in range(3):
         loop(1, 16, lambda j, k=k: g2(peer(j), me16, k).wait_send())
     for xx in range(2):
-        h1(xx).wait_send()
+        loop(0, 4, lambda yy, xx=xx: h1(xx, yy).wait_send())
     loop(1, 8, lambda j: h2((me8 + j) % 8, me8).wait_send())
     loop(1, 4, lambda j: qd(o3i.at[in32(j)], r3i.at[b], g3i_s, g3i_r, j).wait_send())
 
@@ -608,9 +631,10 @@
     def _():
         co3.wait_send()
 
-    loop(1, 4, lambda j: dpc(gda.at[q64(d)], gda.at[q64(d)], da_s, da_r, d, j).wait_send())
-    loop(1, 4, lambda j: dpc(r4i.at[d], r4i.at[d], g4i_s, g4i_r, d, j).wait_send())
-    loop(1, 4, lambda j: dpc(r4o.at[d], r4o.at[d], g4o_s, g4o_r, d, j).wait_send())
+    for c in (tda, t4i, t4o):
+        c["x"].wait_send()
+        c["sib"].wait_send()
+        c["fwd"].wait_send()
 
 
 def finish(side, dprev, gda, gi, go, gg, o_side, o_dprev, o_gdown, o_gin, o_gout, o_gain, o_gate):
@@ -671,7 +695,7 @@
         dma((4, 4)), dma((4, 4)), dma((32,)), dma((32,)), dma((8,)), dma((8,)), dma((2,)), dma((2,)),
         dma((4,)), dma((4,)), dma((8,)), dma((8,)), dma((4,)), dma((4,)), dma((4,)), dma((4,)), dma((4,)), dma((4,)),
         dma((4,)), dma((4,)), dma((4,)), dma((4,)), dma((4,)), dma((4,)), dma((8,)), dma((8,)),
-        dma((2,)), dma((2,)), dma((8,)), dma((8,)), dma((4,)), dma((4,)),
+        dma((2, 4)), dma((2, 4)), dma((8,)), dma((8,)), dma((4,)), dma((4,)),
         dma((2, 2)), dma((2, 2)), dma((16,)), dma((16,)), dma((16,)), dma((16,)), dma((4,)), dma((4,)), dma, dma,
         dma((4,)), dma((4,)), dma((4,)), dma((4,)), dma((4,)), dma((4,)), dma, dma, dma((16,)), dma((16,)),
     ]

time: 122 us -> 117 us (0.959); the launches traced: 120 us -> 116 us
  Pallas kernels: 119 us -> 116 us
    pallas_call x1, Pallas kernels: 117 us -> 113 us  [body(): pl.pallas_call(kernel, out_shape=(jax.ShapeDtypeStruct((32, SIDE), BF16),...]
where the time goes in v4:
time: 117 us; the launch traced here: 116 us
  Pallas kernels  116 us (99%)
    pallas_call x1, Pallas kernels, body(): pl.pallas_call(kernel, out_shape=(jax.ShapeDtypeStruct((32, SIDE), BF16),...  113 us
    pallas_call x1, Pallas kernels, body(): pl.pallas_call(finish, out_shape=(jax.ShapeDtypeStruct((32, SIDE), BF16),...  2.4 us

profile of v4, /device:TPU:1, one launch (start us, length us, event | category | flops | bytes accessed | tf_op | source)
XLA Modules:
  0.0 116.4 jit_solution(5958714984159095107)
XLA Ops:
  0.6 113.3 %shard_map.189 = (bf16[32,1024]{1,0:T(8,128)(2,1)}, bf16[32,1024]{1,0:T(8,128)(2,1)}, bf16[256,1024]{1,0:T(8,128)(2,1)}, bf16[4,4,32,128]{3,2,1,0:T(8,128)(2,1)}...) custom-call(bf16[1024,8192]{1,0:T(8,128)(2,1)} %x_hbm.1, bf16[8192,256]{1,0:T(8,128)(2,1)} %wq_hbm.1, ...), custom_call_target="tpu_custom_call" | custom-call | tf_op jit(solution)/shard_map/pallas_call | solution.py:702
  113.9 2.4 %shard_map.190 = (bf16[32,1024]{1,0:T(8,128)(2,1)}, bf16[32,1024]{1,0:T(8,128)(2,1)}, f32[256,1024]{1,0:T(8,128)}, f32[32,1792]{1,0:T(8,128)}, f32[56,1024]{1,0:...) custom-call(bf16[32,1024]{1,0:T(8,128)(2,1)} %get-tuple-element.20.side, bf16[32,1024]{1,0:T(8,128)(2,1)} %get-tuple-element.21.dprev, ...), custom_call_target="tpu_custom_call" | custom-call | tf_op jit(solution)/shard_map/pallas_call | solution.py:722
